TPU v7x, 128 devices: a whole 4x4x4 slice. The times are simulated.
128 devices in a mesh: prompt: 8 (over z_hi, y), group: 16 (over x, z_lo, core).
Axes of the slice: x: 4, y: 4, z: 4 (z_hi: 2, z_lo: 2; z = z_hi * 2 + z_lo), core: 2. Of those that a mesh axis runs over, the one named last changes fastest.
Arguments:
- prompt_q: bfloat16 [2048, 1024], P(('prompt', 'group')), may hold values from -6 to 6
- prompt_k: bfloat16 [2048, 1024], P(('prompt', 'group')), may hold values from -6 to 6
- prompt_v: bfloat16 [2048, 1024], P(('prompt', 'group')), may hold values from -6 to 6
- prompt_grad: bfloat16 [2048, 1024], P(('prompt', 'group')), may hold values from -6 to 6
- cont_q: bfloat16 [16, 2048, 1024], P('group', None, 'prompt'), may hold values from -6 to 6
- cont_k: bfloat16 [16, 2048, 1024], P('group', None, 'prompt'), may hold values from -6 to 6
- cont_v: bfloat16 [16, 2048, 1024], P('group', None, 'prompt'), may hold values from -6 to 6
- cont_grad: bfloat16 [16, 2048, 1024], P('group', None, 'prompt'), may hold values from -6 to 6
- lengths: int32 [16], P('group'), may hold values from 256 to 2048, as said below
Outputs:
- prompt_dq: bfloat16 [2048, 1024], P(('prompt', 'group'))
- prompt_dk: bfloat16 [2048, 1024], P(('prompt', 'group'))
- prompt_dv: bfloat16 [2048, 1024], P(('prompt', 'group'))
- cont_dq: bfloat16 [16, 2048, 1024], P('group', None, 'prompt')
- cont_dk: bfloat16 [16, 2048, 1024], P('group', None, 'prompt')
- cont_dv: bfloat16 [16, 2048, 1024], P('group', None, 'prompt')
Inputs may be any that keep to these rules, and one draw needn't show every extreme that they name: `lengths`: one member's continuation fills all 2048 rows.
All inputs are finite; a program needn't handle non-finite values.
Results may differ from a plain program's by a relative error of at most 0.024.
Values may be sent and summed in bfloat16 or wider, within the bound.
A program may use at most 64 MiB of HBM per device.

v0:
```python
import jax
import jax.numpy as jnp
from jax import lax
from jax.sharding import PartitionSpec as P

HEAD_SIZE = 128


def masked_scores(query_heads, key_heads, query_pos, key_pos):
    scaling = HEAD_SIZE ** (-0.5)
    scores = (
        jnp.einsum("qhd,khd->hqk", query_heads, key_heads, preferred_element_type=jnp.float32)
        * scaling
    )
    visible = key_pos[None, :] <= query_pos[:, None]
    return jnp.where(visible[None], scores, -jnp.inf)


def forward_block(query_heads, grad_heads, query_pos, key_heads, value_heads, key_pos):
    scores = masked_scores(query_heads, key_heads, query_pos, key_pos)
    row_max = jnp.max(scores, axis=2, keepdims=True)
    shifted = jnp.exp(scores - row_max)
    row_sum = jnp.sum(shifted, axis=2, keepdims=True)
    attn_probs = shifted / row_sum
    probs_low = attn_probs.astype(jnp.bfloat16)
    output = jnp.einsum("hqk,khd->qhd", probs_low, value_heads, preferred_element_type=jnp.float32)
    row_delta = jnp.einsum("qhd,qhd->hq", grad_heads.astype(jnp.float32), output)[:, :, None]
    return (row_max, row_sum, row_delta, attn_probs, probs_low)


def gradients(
    attn_probs, probs_low, query_heads, grad_heads, key_heads, value_heads, row_delta, live_rows
):
    scaling = HEAD_SIZE ** (-0.5)
    dprob = jnp.einsum("qhd,khd->hqk", grad_heads, value_heads, preferred_element_type=jnp.float32)
    keep = live_rows[None, :, None]
    dscore = jnp.where(keep, attn_probs * (dprob - row_delta), 0.0)
    dscore_low = dscore.astype(jnp.bfloat16)
    live_probs = jnp.where(keep, probs_low, jnp.zeros_like(probs_low))
    grad_query = (
        jnp.einsum("hqk,khd->qhd", dscore_low, key_heads, preferred_element_type=jnp.float32)
        * scaling
    )
    grad_key = (
        jnp.einsum("hqk,qhd->khd", dscore_low, query_heads, preferred_element_type=jnp.float32)
        * scaling
    )
    grad_value = jnp.einsum(
        "hqk,qhd->khd", live_probs, grad_heads, preferred_element_type=jnp.float32
    )
    return (grad_query, grad_key, grad_value)


def guarded(kernel, operands):
    return kernel(*operands)


def reduce_prompt(grad_key, grad_value, layout):
    key_low = grad_key.astype(jnp.bfloat16).reshape(layout)
    value_low = grad_value.astype(jnp.bfloat16).reshape(layout)
    summed = (
        lax.psum_scatter(key_low, "group", scatter_dimension=0, tiled=True).astype(jnp.float32),
        lax.psum_scatter(value_low, "group", scatter_dimension=0, tiled=True).astype(jnp.float32),
    )
    return (summed[0][0].astype(jnp.bfloat16), summed[1][0].astype(jnp.bfloat16))


def shards(prompt_q, prompt_k, prompt_v, prompt_grad, cont_q, cont_k, cont_v, cont_grad, lengths):
    n_prompt = lax.axis_size("prompt")
    n_group = lax.axis_size("group")
    shard_rows = prompt_q.shape[0]
    columns = cont_q.shape[2]
    per_device = columns // HEAD_SIZE
    cont_span = cont_q.shape[1]
    prompt_total = shard_rows * n_prompt * n_group
    prompt_part = n_prompt * shard_rows
    paired = jnp.stack([prompt_k, prompt_v])[:, None]
    block_pair = lax.all_gather(paired, "group", axis=1, tiled=True)
    block_pair = block_pair.reshape(2, n_group, 1, shard_rows, n_prompt, columns)
    head_pair = lax.all_to_all(block_pair, "prompt", split_axis=4, concat_axis=2, tiled=True)
    query_pair = jnp.stack([prompt_q, prompt_grad]).reshape(2, shard_rows, n_prompt, columns)
    query_pair = lax.all_to_all(query_pair, "prompt", split_axis=2, concat_axis=1, tiled=True)
    query_rows = query_pair[0].reshape(prompt_part, columns)
    grad_rows = query_pair[1].reshape(prompt_part, columns)
    key_rows = head_pair[0].reshape(prompt_total, columns)
    value_rows = head_pair[1].reshape(prompt_total, columns)
    group_index = lax.axis_index("group")
    key_grid = (
        jnp.arange(n_group, dtype=jnp.int32)[:, None, None] * shard_rows
        + jnp.arange(n_prompt, dtype=jnp.int32)[None, :, None] * (n_group * shard_rows)
        + jnp.arange(shard_rows, dtype=jnp.int32)[None, None, :]
    )
    prompt_query_pos = (
        jnp.arange(n_prompt, dtype=jnp.int32)[:, None] * (n_group * shard_rows)
        + group_index * shard_rows
        + jnp.arange(shard_rows, dtype=jnp.int32)[None, :]
    )
    cont_pos = prompt_total + jnp.arange(cont_span, dtype=jnp.int32)
    key_pos = jnp.concatenate([key_grid.reshape(-1), cont_pos])
    query_pos = jnp.concatenate([prompt_query_pos.reshape(-1), cont_pos])
    live_rows = jnp.concatenate(
        [jnp.ones((prompt_part,), dtype=bool), jnp.arange(cont_span, dtype=jnp.int32) < lengths[0]]
    )
    key_heads = jnp.concatenate([key_rows, cont_k[0]]).reshape(-1, per_device, HEAD_SIZE)
    value_heads = jnp.concatenate([value_rows, cont_v[0]]).reshape(-1, per_device, HEAD_SIZE)
    query_heads = jnp.concatenate([query_rows, cont_q[0]]).reshape(-1, per_device, HEAD_SIZE)
    grad_heads = jnp.concatenate([grad_rows, cont_grad[0]]).reshape(-1, per_device, HEAD_SIZE)
    query_count = query_heads.shape[0]
    blocks = max(1, query_count // 512)
    while query_count % blocks:
        blocks -= 1
    block_rows = query_count // blocks
    block_items = (
        query_heads.reshape(blocks, block_rows, per_device, HEAD_SIZE),
        grad_heads.reshape(blocks, block_rows, per_device, HEAD_SIZE),
        query_pos.reshape(blocks, block_rows),
        live_rows.reshape(blocks, block_rows),
    )
    layout = (n_group, n_prompt, shard_rows, columns)
    empty_sums = jnp.zeros(key_heads.shape, jnp.float32)

    def joint_step(running, block_item):

        def kernel(query_block, grad_block, pos_block, live_block):
            row_max, row_sum, row_delta, attn_probs, probs_low = forward_block(
                query_block, grad_block, pos_block, key_heads, value_heads, key_pos
            )
            return gradients(
                attn_probs,
                probs_low,
                query_block,
                grad_block,
                key_heads,
                value_heads,
                row_delta,
                live_block,
            )

        grad_query, grad_key, grad_value = guarded(kernel, block_item)
        return ((running[0] + grad_key, running[1] + grad_value), grad_query)

    sums_pair, query_grads = lax.scan(joint_step, (empty_sums, empty_sums), block_items)
    prompt_dk, prompt_dv = reduce_prompt(
        sums_pair[0][:prompt_total], sums_pair[1][:prompt_total], layout
    )
    cont_key_sums = sums_pair[0][prompt_total:]
    cont_value_sums = sums_pair[1][prompt_total:]
    query_grads = query_grads.reshape(query_count, columns)
    prompt_dq = (
        query_grads[:prompt_part].astype(jnp.bfloat16).reshape(n_prompt, shard_rows, 1, columns)
    )
    returned = (
        lax.all_to_all(prompt_dq, "prompt", split_axis=0, concat_axis=2, tiled=True),
        lax.all_to_all(
            prompt_dk.reshape(n_prompt, shard_rows, 1, columns),
            "prompt",
            split_axis=0,
            concat_axis=2,
            tiled=True,
        ),
        lax.all_to_all(
            prompt_dv.reshape(n_prompt, shard_rows, 1, columns),
            "prompt",
            split_axis=0,
            concat_axis=2,
            tiled=True,
        ),
    )
    out_dq = returned[0].reshape(shard_rows, n_prompt * columns)
    out_dk = returned[1].reshape(shard_rows, n_prompt * columns)
    out_dv = returned[2].reshape(shard_rows, n_prompt * columns)
    cont_dq = query_grads[prompt_part:].astype(jnp.bfloat16).reshape(1, cont_span, columns)
    cont_dk = cont_key_sums.astype(jnp.bfloat16).reshape(1, cont_span, columns)
    cont_dv = cont_value_sums.astype(jnp.bfloat16).reshape(1, cont_span, columns)
    return (out_dq, out_dk, out_dv, cont_dq, cont_dk, cont_dv)


def solution(mesh):
    return jax.shard_map(
        shards,
        mesh=mesh,
        in_specs=(
            P(("prompt", "group"), None),
            P(("prompt", "group"), None),
            P(("prompt", "group"), None),
            P(("prompt", "group"), None),
            P("group", None, "prompt"),
            P("group", None, "prompt"),
            P("group", None, "prompt"),
            P("group", None, "prompt"),
            P("group"),
        ),
        out_specs=(
            P(("prompt", "group"), None),
            P(("prompt", "group"), None),
            P(("prompt", "group"), None),
            P("group", None, "prompt"),
            P("group", None, "prompt"),
            P("group", None, "prompt"),
        ),
        check_vma=False,
    )
```

profile of v0, /device:TPU:1, one launch (start us, length us, event | category | flops | bytes accessed | tf_op | source)
XLA Modules:
  0.0 319.4 jit_solution(9548671172758423343)
XLA Ops:
  10.8 8.3 %all-to-all-start = ((bf16[2,16,8,128]{3,1,0,2:T(8,128)(2,1)}), bf16[2,16,8,128]{3,1,0,2:T(8,128)(2,1)S(1)}, u32[]{:S(2)}, u32[]{:S(2)}) async-start(bf16[2,16,8,128]{3,1,0,2:T(8,128)(2,1)} %copy.39), calls=%async_computation | async-start | bytes 131072 | tf_op jit(solution)/shard_map/all_to_all | solution.py:82
  20.5 25.8 %all-gather.3.cloned.1.call-done = bf16[2,256,1024]{2,1,0:T(8,128)(2,1)} async-done(((bf16[2,16,1024]{2,1,0:T(8,128)(2,1)}), bf16[2,256,1024]{2,1,0:T(8,128)(2,1)}) %all-gather.3.cloned.1.call-update) | async-done | bytes 1048592 | tf_op jit(solution)/shard_map/all_gather | solution.py:78
  49.0 6.3 %all-to-all-start.1 = ((bf16[2,16,1,16,8,128]{5,3,1,0,2,4:T(8,128)(2,1)}), bf16[2,16,1,16,8,128]{5,3,1,0,2,4:T(8,128)(2,1)S(1)}, u32[]{:S(2)}, u32[]{:S(2)}) async-start(bf16[2,16,1,16,8,128]{5,3,1,0,2,4:T(8,128)(2,1)} %copy.40), calls=%async_computation.1 | async-start | bytes 2097152 | tf_op jit(solution)/shard_map/all_to_all | solution.py:80
  59.2 13.5 %all-to-all-done.1 = bf16[2,16,1,16,8,128]{5,3,1,0,2,4:T(8,128)(2,1)S(1)} async-done(((bf16[2,16,1,16,8,128]{5,3,1,0,2,4:T(8,128)(2,1)}), bf16[2,16,1,16,8,128]{5,3,1,0,2,4:T(8,128)(2,1)S(1)}, u32[]{:S(2)}, u32[]{:S(2)}) %all-to-all-start.1) | async-done | bytes 1048608 | tf_op jit(solution)/shard_map/all_to_all | solution.py:80
  75.1 106.3 %while.15 = (s32[]{:T(128)}, f32[4096,1,128]{0,2,1:T(8,128)}, f32[4096,1,128]{0,2,1:T(8,128)S(1)}, bf16[4,544,1,128]{3,1,2,0:T(8,128)(2,1)}, bf16[4,544,1,128]{3...) while((s32[]{:T(128)}, f32[4096,1,128]{0,2,1:T(8,128)}, ...), condition=%wide.region_3.4_spmd.clone, body=%wide.region_0.3_spmd.clone.sunk | while | flops 3458873856 | bytes 160401104 | solution.py:142
  75.1 3.0 fusion.68
  81.3 2.5 fusion.71
  84.7 4.5 %select_convert_fusion.2 = bf16[544,4096]{1,0:T(8,128)(2,1)} fusion(f32[544,4096]{1,0:T(8,128)S(1)} %fusion.70, f32[544]{0:T(1024)S(1)} %fusion.71, pred[544]{0:T(1024)(128)(4,1)S(1)} %dynamic-slice_reduce_fusion.5, bf16[4096,1,128]{2,0,1:T(8,128)(2,1)S(1)} %get-tuple-element.278, bf16[4,544,1,128]{3,1,2,0:T(8,128)(2,1)} %get-tuple-element.277, ...), kind=kOutput, calls=%fused_computation.clone.1 | convolution fusion | flops 579338240 | bytes 14560416 | tf_op jit(solution)/shard_map/while/body/eval_jaxpr/qhd,khd->hqk/dot_general | solution.py:35
  89.2 4.8 %fusion.72 = f32[4096,1,128]{0,2,1:T(8,128)} fusion(bf16[544,4096]{1,0:T(8,128)(2,1)} %select_convert_fusion.2, f32[4096,1,128]{0,2,1:T(8,128)} %get-tuple-element.256, pred[]{:T(512)S(6)} %compare.4, bf16[4,544,1,128]{3,1,2,0:T(8,128)(2,1)} %get-tuple-element.272, s32[]{:T(128)} %get-tuple-element.255), kind=kOutput, calls=%fused_computation.8.clone.1 | convolution fusion | flops 571998208 | bytes 8790529 | tf_op jit(solution)/shard_map/while/body/eval_jaxpr/hqk,qhd->khd/dot_general | solution.py:45
  94.1 3.9 %fusion.74 = bf16[4,544,1,128]{3,1,2,0:T(8,128)(2,1)S(1)} fusion(bf16[4,544,1,128]{3,1,2,0:T(8,128)(2,1)S(1)} %copy-done.2, s32[]{:T(128)} %get-tuple-element.255, bf16[544,4096]{1,0:T(8,128)(2,1)} %select_convert_fusion.2, bf16[4096,1,128]{2,0,1:T(8,128)(2,1)S(1)} %copy-done.1), kind=kOutput, calls=%fused_computation.18.clone.1 | convolution fusion | flops 570494976 | bytes 5783556 | tf_op jit(solution)/shard_map/while/body/eval_jaxpr/hqk,khd->qhd/dot_general | solution.py:41
  101.2 3.0 fusion.68
  107.4 2.5 fusion.71
  110.9 4.5 %select_convert_fusion.2 = bf16[544,4096]{1,0:T(8,128)(2,1)} fusion(f32[544,4096]{1,0:T(8,128)S(1)} %fusion.70, f32[544]{0:T(1024)S(1)} %fusion.71, pred[544]{0:T(1024)(128)(4,1)S(1)} %dynamic-slice_reduce_fusion.5, bf16[4096,1,128]{2,0,1:T(8,128)(2,1)S(1)} %get-tuple-element.278, bf16[4,544,1,128]{3,1,2,0:T(8,128)(2,1)} %get-tuple-element.277, ...), kind=kOutput, calls=%fused_computation.clone.1 | convolution fusion | flops 579338240 | bytes 14560416 | tf_op jit(solution)/shard_map/while/body/eval_jaxpr/qhd,khd->hqk/dot_general | solution.py:35
  115.4 5.5 %fusion.72 = f32[4096,1,128]{0,2,1:T(8,128)} fusion(bf16[544,4096]{1,0:T(8,128)(2,1)} %select_convert_fusion.2, f32[4096,1,128]{0,2,1:T(8,128)} %get-tuple-element.256, pred[]{:T(512)S(6)} %compare.4, bf16[4,544,1,128]{3,1,2,0:T(8,128)(2,1)} %get-tuple-element.272, s32[]{:T(128)} %get-tuple-element.255), kind=kOutput, calls=%fused_computation.8.clone.1 | convolution fusion | flops 571998208 | bytes 8790529 | tf_op jit(solution)/shard_map/while/body/eval_jaxpr/hqk,qhd->khd/dot_general | solution.py:45
  120.9 3.8 %fusion.74 = bf16[4,544,1,128]{3,1,2,0:T(8,128)(2,1)S(1)} fusion(bf16[4,544,1,128]{3,1,2,0:T(8,128)(2,1)S(1)} %copy-done.2, s32[]{:T(128)} %get-tuple-element.255, bf16[544,4096]{1,0:T(8,128)(2,1)} %select_convert_fusion.2, bf16[4096,1,128]{2,0,1:T(8,128)(2,1)S(1)} %copy-done.1), kind=kOutput, calls=%fused_computation.18.clone.1 | convolution fusion | flops 570494976 | bytes 5783556 | tf_op jit(solution)/shard_map/while/body/eval_jaxpr/hqk,khd->qhd/dot_general | solution.py:41
  128.0 3.0 fusion.68
  134.2 2.5 fusion.71
  137.6 4.5 %select_convert_fusion.2 = bf16[544,4096]{1,0:T(8,128)(2,1)} fusion(f32[544,4096]{1,0:T(8,128)S(1)} %fusion.70, f32[544]{0:T(1024)S(1)} %fusion.71, pred[544]{0:T(1024)(128)(4,1)S(1)} %dynamic-slice_reduce_fusion.5, bf16[4096,1,128]{2,0,1:T(8,128)(2,1)S(1)} %get-tuple-element.278, bf16[4,544,1,128]{3,1,2,0:T(8,128)(2,1)} %get-tuple-element.277, ...), kind=kOutput, calls=%fused_computation.clone.1 | convolution fusion | flops 579338240 | bytes 14560416 | tf_op jit(solution)/shard_map/while/body/eval_jaxpr/qhd,khd->hqk/dot_general | solution.py:35
  142.1 5.5 %fusion.72 = f32[4096,1,128]{0,2,1:T(8,128)} fusion(bf16[544,4096]{1,0:T(8,128)(2,1)} %select_convert_fusion.2, f32[4096,1,128]{0,2,1:T(8,128)} %get-tuple-element.256, pred[]{:T(512)S(6)} %compare.4, bf16[4,544,1,128]{3,1,2,0:T(8,128)(2,1)} %get-tuple-element.272, s32[]{:T(128)} %get-tuple-element.255), kind=kOutput, calls=%fused_computation.8.clone.1 | convolution fusion | flops 571998208 | bytes 8790529 | tf_op jit(solution)/shard_map/while/body/eval_jaxpr/hqk,qhd->khd/dot_general | solution.py:45
  147.6 3.8 %fusion.74 = bf16[4,544,1,128]{3,1,2,0:T(8,128)(2,1)S(1)} fusion(bf16[4,544,1,128]{3,1,2,0:T(8,128)(2,1)S(1)} %copy-done.2, s32[]{:T(128)} %get-tuple-element.255, bf16[544,4096]{1,0:T(8,128)(2,1)} %select_convert_fusion.2, bf16[4096,1,128]{2,0,1:T(8,128)(2,1)S(1)} %copy-done.1), kind=kOutput, calls=%fused_computation.18.clone.1 | convolution fusion | flops 570494976 | bytes 5783556 | tf_op jit(solution)/shard_map/while/body/eval_jaxpr/hqk,khd->qhd/dot_general | solution.py:41
  152.3 2.4 fusion.73
  154.7 3.0 fusion.68
  160.9 2.5 fusion.71
  164.3 4.5 %select_convert_fusion.2 = bf16[544,4096]{1,0:T(8,128)(2,1)} fusion(f32[544,4096]{1,0:T(8,128)S(1)} %fusion.70, f32[544]{0:T(1024)S(1)} %fusion.71, pred[544]{0:T(1024)(128)(4,1)S(1)} %dynamic-slice_reduce_fusion.5, bf16[4096,1,128]{2,0,1:T(8,128)(2,1)S(1)} %get-tuple-element.278, bf16[4,544,1,128]{3,1,2,0:T(8,128)(2,1)} %get-tuple-element.277, ...), kind=kOutput, calls=%fused_computation.clone.1 | convolution fusion | flops 579338240 | bytes 14560416 | tf_op jit(solution)/shard_map/while/body/eval_jaxpr/qhd,khd->hqk/dot_general | solution.py:35
  168.9 5.5 %fusion.72 = f32[4096,1,128]{0,2,1:T(8,128)} fusion(bf16[544,4096]{1,0:T(8,128)(2,1)} %select_convert_fusion.2, f32[4096,1,128]{0,2,1:T(8,128)} %get-tuple-element.256, pred[]{:T(512)S(6)} %compare.4, bf16[4,544,1,128]{3,1,2,0:T(8,128)(2,1)} %get-tuple-element.272, s32[]{:T(128)} %get-tuple-element.255), kind=kOutput, calls=%fused_computation.8.clone.1 | convolution fusion | flops 571998208 | bytes 8790529 | tf_op jit(solution)/shard_map/while/body/eval_jaxpr/hqk,qhd->khd/dot_general | solution.py:45
  174.3 3.8 %fusion.74 = bf16[4,544,1,128]{3,1,2,0:T(8,128)(2,1)S(1)} fusion(bf16[4,544,1,128]{3,1,2,0:T(8,128)(2,1)S(1)} %copy-done.2, s32[]{:T(128)} %get-tuple-element.255, bf16[544,4096]{1,0:T(8,128)(2,1)} %select_convert_fusion.2, bf16[4096,1,128]{2,0,1:T(8,128)(2,1)S(1)} %copy-done.1), kind=kOutput, calls=%fused_computation.18.clone.1 | convolution fusion | flops 570494976 | bytes 5783556 | tf_op jit(solution)/shard_map/while/body/eval_jaxpr/hqk,khd->qhd/dot_general | solution.py:41
  186.2 9.0 %all_to_all.75 = bf16[8,16,1,128]{3,1,2,0:T(8,128)(2,1)S(1)} all-to-all(bf16[8,16,1,128]{3,1,2,0:T(8,128)(2,1)S(1)} %bitcast.181), channel_id=1, replica_groups=mesh['prompt'=8,'group'=16] {'prompt'}, dimensions={0} | all-to-all | bytes 65536 | tf_op jit(solution)/shard_map/all_to_all | solution.py:153
  195.2 41.5 %reduce-scatter.5.cloned.1.call-done = bf16[1,8,16,128]{3,2,1,0:T(8,128)(2,1)} async-done(((bf16[16,8,16,128]{3,2,1,0:T(8,128)(2,1)}), bf16[1,8,16,128]{3,2,1,0:T(8,128)(2,1)}) %reduce-scatter.5.cloned.1.call-update) | async-done | bytes 32784 | tf_op jit(solution)/shard_map/reduce_scatter | solution.py:63
  236.7 6.8 %all-to-all-start.4 = ((bf16[8,16,1,128]{3,1,2,0:T(8,128)(2,1)}), bf16[8,16,1,128]{3,1,2,0:T(8,128)(2,1)S(1)}, u32[]{:S(2)}, u32[]{:S(2)}) async-start(bf16[8,16,1,128]{3,1,2,0:T(8,128)(2,1)} %bitcast.187), calls=%async_computation.6 | async-start | bytes 65536 | tf_op jit(solution)/shard_map/all_to_all | solution.py:161
  243.5 55.4 %reduce-scatter.3.cloned.1.call-done = bf16[1,8,16,128]{3,2,1,0:T(8,128)(2,1)} async-done(((bf16[16,8,16,128]{3,2,1,0:T(8,128)(2,1)}), bf16[1,8,16,128]{3,2,1,0:T(8,128)(2,1)}) %reduce-scatter.3.cloned.1.call-update) | async-done | bytes 32784 | tf_op jit(solution)/shard_map/reduce_scatter | solution.py:62
  298.9 6.7 %all-to-all-start.3 = ((bf16[8,16,1,128]{3,1,2,0:T(8,128)(2,1)}), bf16[8,16,1,128]{3,1,2,0:T(8,128)(2,1)S(1)}, u32[]{:S(2)}, u32[]{:S(2)}) async-start(bf16[8,16,1,128]{3,1,2,0:T(8,128)(2,1)} %bitcast.186), calls=%async_computation.4 | async-start | bytes 65536 | tf_op jit(solution)/shard_map/all_to_all | solution.py:154
  307.7 4.5 %all-to-all-done.3 = bf16[8,16,1,128]{3,1,2,0:T(8,128)(2,1)S(1)} async-done(((bf16[8,16,1,128]{3,1,2,0:T(8,128)(2,1)}), bf16[8,16,1,128]{3,1,2,0:T(8,128)(2,1)S(1)}, u32[]{:S(2)}, u32[]{:S(2)}) %all-to-all-start.3) | async-done | bytes 32800 | tf_op jit(solution)/shard_map/all_to_all | solution.py:154
  (137 shorter events, 47.5 us)
Async XLA Ops:
  7.2 39.2 %all-gather.3.cloned.1.call-start = ((), (), s32[]{:S(2)}) async-start(), calls=%async_computation.9 | async-start | bytes 1114112 | tf_op jit(solution)/shard_map/all_gather | solution.py:78
  10.8 38.2 %all-to-all-start = ((bf16[2,16,8,128]{3,1,0,2:T(8,128)(2,1)}), bf16[2,16,8,128]{3,1,0,2:T(8,128)(2,1)S(1)}, u32[]{:S(2)}, u32[]{:S(2)}) async-start(bf16[2,16,8,128]{3,1,0,2:T(8,128)(2,1)} %copy.39), calls=%async_computation | async-start | bytes 131072 | tf_op jit(solution)/shard_map/all_to_all | solution.py:82
  49.0 23.7 %all-to-all-start.1 = ((bf16[2,16,1,16,8,128]{5,3,1,0,2,4:T(8,128)(2,1)}), bf16[2,16,1,16,8,128]{5,3,1,0,2,4:T(8,128)(2,1)S(1)}, u32[]{:S(2)}, u32[]{:S(2)}) async-start(bf16[2,16,1,16,8,128]{5,3,1,0,2,4:T(8,128)(2,1)} %copy.40), calls=%async_computation.1 | async-start | bytes 2097152 | tf_op jit(solution)/shard_map/all_to_all | solution.py:80
  55.4 181.3 %reduce-scatter.5.cloned.1.call-start = ((), (), s32[]{:S(2)}) async-start(), calls=%async_computation.8 | async-start | bytes 557056 | tf_op jit(solution)/shard_map/reduce_scatter | solution.py:63
  81.3 3.5 %copy-start = (f32[544,4096]{1,0:T(8,128)}, f32[544,4096]{1,0:T(8,128)S(1)}, u32[]{:S(2)}) copy-start(f32[544,4096]{1,0:T(8,128)S(1)} %fusion.70) | copy-start | bytes 26738692 | tf_op jit(solution)/shard_map/while
  89.2 4.8 %copy-start.1 = (bf16[4096,1,128]{2,0,1:T(8,128)(2,1)S(1)}, bf16[4096,1,128]{2,0,1:T(8,128)(2,1)}, u32[]{:S(2)}) copy-start(bf16[4096,1,128]{2,0,1:T(8,128)(2,1)} %get-tuple-element.276) | copy-start | bytes 3145732 | tf_op jit(solution)/shard_map/while
  89.2 4.8 %copy-start.2 = (bf16[4,544,1,128]{3,1,2,0:T(8,128)(2,1)S(1)}, bf16[4,544,1,128]{3,1,2,0:T(8,128)(2,1)}, u32[]{:S(2)}) copy-start(bf16[4,544,1,128]{3,1,2,0:T(8,128)(2,1)} %get-tuple-element.258) | copy-start | bytes 1671172 | tf_op jit(solution)/shard_map/while
  89.2 9.5 %slice-start = ((s8[8912896]{0:T(1024)(128)(4,1)}), s8[4194304]{0:T(1024)(128)(4,1)S(1)}, s32[]{:S(2)}) async-start(s8[8912896]{0:T(1024)(128)(4,1)} %bitcast.155), calls=%async_computation.10 | async-start | bytes 8388608 | tf_op jit(solution)/shard_map/while
  89.2 9.5 %slice-start.1 = ((s8[8912896]{0:T(1024)(128)(4,1)}), s8[4194304]{0:T(1024)(128)(4,1)S(1)}, s32[]{:S(2)}) async-start(s8[8912896]{0:T(1024)(128)(4,1)} %bitcast.155), calls=%async_computation.11 | async-start | bytes 8388608 | tf_op jit(solution)/shard_map/while
  94.1 4.7 %slice-start.2 = ((s8[8912896]{0:T(1024)(128)(4,1)}), s8[524288]{0:T(1024)(128)(4,1)S(1)}, s32[]{:S(2)}) async-start(s8[8912896]{0:T(1024)(128)(4,1)} %bitcast.155), calls=%async_computation.12 | async-start | bytes 1048576 | tf_op jit(solution)/shard_map/while
  107.4 3.5 %copy-start = (f32[544,4096]{1,0:T(8,128)}, f32[544,4096]{1,0:T(8,128)S(1)}, u32[]{:S(2)}) copy-start(f32[544,4096]{1,0:T(8,128)S(1)} %fusion.70) | copy-start | bytes 26738692 | tf_op jit(solution)/shard_map/while
  115.4 5.5 %copy-start.1 = (bf16[4096,1,128]{2,0,1:T(8,128)(2,1)S(1)}, bf16[4096,1,128]{2,0,1:T(8,128)(2,1)}, u32[]{:S(2)}) copy-start(bf16[4096,1,128]{2,0,1:T(8,128)(2,1)} %get-tuple-element.276) | copy-start | bytes 3145732 | tf_op jit(solution)/shard_map/while
  115.4 5.5 %copy-start.2 = (bf16[4,544,1,128]{3,1,2,0:T(8,128)(2,1)S(1)}, bf16[4,544,1,128]{3,1,2,0:T(8,128)(2,1)}, u32[]{:S(2)}) copy-start(bf16[4,544,1,128]{3,1,2,0:T(8,128)(2,1)} %get-tuple-element.258) | copy-start | bytes 1671172 | tf_op jit(solution)/shard_map/while
  115.4 10.1 %slice-start = ((s8[8912896]{0:T(1024)(128)(4,1)}), s8[4194304]{0:T(1024)(128)(4,1)S(1)}, s32[]{:S(2)}) async-start(s8[8912896]{0:T(1024)(128)(4,1)} %bitcast.155), calls=%async_computation.10 | async-start | bytes 8388608 | tf_op jit(solution)/shard_map/while
  115.4 10.1 %slice-start.1 = ((s8[8912896]{0:T(1024)(128)(4,1)}), s8[4194304]{0:T(1024)(128)(4,1)S(1)}, s32[]{:S(2)}) async-start(s8[8912896]{0:T(1024)(128)(4,1)} %bitcast.155), calls=%async_computation.11 | async-start | bytes 8388608 | tf_op jit(solution)/shard_map/while
  120.9 4.7 %slice-start.2 = ((s8[8912896]{0:T(1024)(128)(4,1)}), s8[524288]{0:T(1024)(128)(4,1)S(1)}, s32[]{:S(2)}) async-start(s8[8912896]{0:T(1024)(128)(4,1)} %bitcast.155), calls=%async_computation.12 | async-start | bytes 1048576 | tf_op jit(solution)/shard_map/while
  134.2 3.5 %copy-start = (f32[544,4096]{1,0:T(8,128)}, f32[544,4096]{1,0:T(8,128)S(1)}, u32[]{:S(2)}) copy-start(f32[544,4096]{1,0:T(8,128)S(1)} %fusion.70) | copy-start | bytes 26738692 | tf_op jit(solution)/shard_map/while
  142.1 5.5 %copy-start.1 = (bf16[4096,1,128]{2,0,1:T(8,128)(2,1)S(1)}, bf16[4096,1,128]{2,0,1:T(8,128)(2,1)}, u32[]{:S(2)}) copy-start(bf16[4096,1,128]{2,0,1:T(8,128)(2,1)} %get-tuple-element.276) | copy-start | bytes 3145732 | tf_op jit(solution)/shard_map/while
  142.1 5.5 %copy-start.2 = (bf16[4,544,1,128]{3,1,2,0:T(8,128)(2,1)S(1)}, bf16[4,544,1,128]{3,1,2,0:T(8,128)(2,1)}, u32[]{:S(2)}) copy-start(bf16[4,544,1,128]{3,1,2,0:T(8,128)(2,1)} %get-tuple-element.258) | copy-start | bytes 1671172 | tf_op jit(solution)/shard_map/while
  142.1 10.1 %slice-start = ((s8[8912896]{0:T(1024)(128)(4,1)}), s8[4194304]{0:T(1024)(128)(4,1)S(1)}, s32[]{:S(2)}) async-start(s8[8912896]{0:T(1024)(128)(4,1)} %bitcast.155), calls=%async_computation.10 | async-start | bytes 8388608 | tf_op jit(solution)/shard_map/while
  142.1 10.1 %slice-start.1 = ((s8[8912896]{0:T(1024)(128)(4,1)}), s8[4194304]{0:T(1024)(128)(4,1)S(1)}, s32[]{:S(2)}) async-start(s8[8912896]{0:T(1024)(128)(4,1)} %bitcast.155), calls=%async_computation.11 | async-start | bytes 8388608 | tf_op jit(solution)/shard_map/while
  147.6 4.7 %slice-start.2 = ((s8[8912896]{0:T(1024)(128)(4,1)}), s8[524288]{0:T(1024)(128)(4,1)S(1)}, s32[]{:S(2)}) async-start(s8[8912896]{0:T(1024)(128)(4,1)} %bitcast.155), calls=%async_computation.12 | async-start | bytes 1048576 | tf_op jit(solution)/shard_map/while
  160.9 3.5 %copy-start = (f32[544,4096]{1,0:T(8,128)}, f32[544,4096]{1,0:T(8,128)S(1)}, u32[]{:S(2)}) copy-start(f32[544,4096]{1,0:T(8,128)S(1)} %fusion.70) | copy-start | bytes 26738692 | tf_op jit(solution)/shard_map/while
  168.8 5.5 %copy-start.1 = (bf16[4096,1,128]{2,0,1:T(8,128)(2,1)S(1)}, bf16[4096,1,128]{2,0,1:T(8,128)(2,1)}, u32[]{:S(2)}) copy-start(bf16[4096,1,128]{2,0,1:T(8,128)(2,1)} %get-tuple-element.276) | copy-start | bytes 3145732 | tf_op jit(solution)/shard_map/while
  168.8 5.5 %copy-start.2 = (bf16[4,544,1,128]{3,1,2,0:T(8,128)(2,1)S(1)}, bf16[4,544,1,128]{3,1,2,0:T(8,128)(2,1)}, u32[]{:S(2)}) copy-start(bf16[4,544,1,128]{3,1,2,0:T(8,128)(2,1)} %get-tuple-element.258) | copy-start | bytes 1671172 | tf_op jit(solution)/shard_map/while
  168.8 10.1 %slice-start = ((s8[8912896]{0:T(1024)(128)(4,1)}), s8[4194304]{0:T(1024)(128)(4,1)S(1)}, s32[]{:S(2)}) async-start(s8[8912896]{0:T(1024)(128)(4,1)} %bitcast.155), calls=%async_computation.10 | async-start | bytes 8388608 | tf_op jit(solution)/shard_map/while
  168.8 10.1 %slice-start.1 = ((s8[8912896]{0:T(1024)(128)(4,1)}), s8[4194304]{0:T(1024)(128)(4,1)S(1)}, s32[]{:S(2)}) async-start(s8[8912896]{0:T(1024)(128)(4,1)} %bitcast.155), calls=%async_computation.11 | async-start | bytes 8388608 | tf_op jit(solution)/shard_map/while
  174.3 4.7 %slice-start.2 = ((s8[8912896]{0:T(1024)(128)(4,1)}), s8[524288]{0:T(1024)(128)(4,1)S(1)}, s32[]{:S(2)}) async-start(s8[8912896]{0:T(1024)(128)(4,1)} %bitcast.155), calls=%async_computation.12 | async-start | bytes 1048576 | tf_op jit(solution)/shard_map/while
  182.1 4.0 %copy-start.4 = (bf16[4,544,1,128]{3,1,2,0:T(8,128)(2,1)S(1)}, bf16[4,544,1,128]{3,1,2,0:T(8,128)(2,1)}, u32[]{:S(2)}) copy-start(bf16[4,544,1,128]{3,1,2,0:T(8,128)(2,1)} %get-tuple-element.65) | copy-start | bytes 1671172
  183.2 115.7 %reduce-scatter.3.cloned.1.call-start = ((), (), s32[]{:S(2)}) async-start(), calls=%async_computation.7 | async-start | bytes 557056 | tf_op jit(solution)/shard_map/reduce_scatter | solution.py:62
  236.7 62.2 %all-to-all-start.4 = ((bf16[8,16,1,128]{3,1,2,0:T(8,128)(2,1)}), bf16[8,16,1,128]{3,1,2,0:T(8,128)(2,1)S(1)}, u32[]{:S(2)}, u32[]{:S(2)}) async-start(bf16[8,16,1,128]{3,1,2,0:T(8,128)(2,1)} %bitcast.187), calls=%async_computation.6 | async-start | bytes 65536 | tf_op jit(solution)/shard_map/all_to_all | solution.py:161
  298.9 13.3 %all-to-all-start.3 = ((bf16[8,16,1,128]{3,1,2,0:T(8,128)(2,1)}), bf16[8,16,1,128]{3,1,2,0:T(8,128)(2,1)S(1)}, u32[]{:S(2)}, u32[]{:S(2)}) async-start(bf16[8,16,1,128]{3,1,2,0:T(8,128)(2,1)} %bitcast.186), calls=%async_computation.4 | async-start | bytes 65536 | tf_op jit(solution)/shard_map/all_to_all | solution.py:154
  (6 other events, 5.5 us)
Sparse Core Ops, SparseCore 0:
  10.2 36.0 all-gather.2
  183.3 53.3 reduce-scatter.4
  239.8 59.1 reduce-scatter.2
where the time goes:
time: 325 us; the launch traced here: 319 us
  waiting for transfers between devices  141 us (43%)
  matrix products  86.2 us (27%)
  starting transfers between devices  28.3 us (9%)
  local copies, waits for them, and re-layouts  20.9 us (6%)
  other arithmetic  19.2 us (6%)
  between operations  14.6 us (4%)
  blocking collectives  8.99 us (3%)
    reduce_scatter x1, waiting for transfers between devices, reduce_prompt(): lax.psum_scatter(key_low, 'group', scatter_dimension=0, tiled=True)  55.4 us
    reduce_scatter x1, waiting for transfers between devices, reduce_prompt(): lax.psum_scatter(value_low, 'group', scatter_dimension=0, tiled=True)  41.5 us
    all_gather x1, waiting for transfers between devices, shards(): block_pair = lax.all_gather(paired, 'group', axis=1, tiled=True)  25.8 us
    dot_general x4, matrix products, gradients(): jnp.einsum('hqk,qhd->khd', dscore_low, query_heads, preferred_element_typ...  21.3 us
    dot_general x4, matrix products, gradients(): jnp.einsum('qhd,khd->hqk', grad_heads, value_heads, preferred_element_typ...  18 us
    dot_general x4, matrix products, gradients(): jnp.einsum('hqk,khd->qhd', dscore_low, key_heads, preferred_element_type=...  15.3 us
    all_to_all x1, waiting for transfers between devices, shards(): lax.all_to_all(block_pair, 'prompt', split_axis=4, concat_axis=2, tiled=T...  13.5 us
    dot_general x4, matrix products, masked_scores(): jnp.einsum('qhd,khd->hqk', query_heads, key_heads, preferred_element_type...  12.1 us
  transfers between devices with their start and end apart: 7, of which 5 were waited for; matrix products, arithmetic and copies ran while one was open for 4% of the time, Pallas kernels for 0%

commit v1 on v0

v1 whole, which is shorter than its diff:
```python
import functools
import math

import jax
import jax.numpy as jnp
from jax import lax
from jax.experimental import pallas as pl
from jax.experimental.pallas import tpu as pltpu
from jax.sharding import PartitionSpec as P

F = jnp.float32
B = jnp.bfloat16
HS = 128
NP = 2048
NC = 2048
QB = 256
NB = NC // QB
PQ = 128
NQ = NC + PQ
HEADS = 8
CHIPS = 8
SCALE = HS**-0.5
SCALE2 = SCALE * math.log2(math.e)
NEG = -1e30


def nt(a, b):
    return lax.dot_general(a, b, (((1,), (1,)), ((), ())), preferred_element_type=F)


def nn(a, b):
    return jnp.dot(a, b, preferred_element_type=F)


def fold(x, op):
    return op(x.reshape(x.shape[0] // 8, 8, x.shape[1]), axis=0)


def rowmax(x):
    return jnp.max(x, axis=0, keepdims=True)


def rowsum(x):
    return jnp.sum(x, axis=0, keepdims=True)


def kernel(
    pq, pk, pv, pg, cq, ck, cv, cg, lens,
    o_pdq, o_pdk, o_pdv, o_dq, o_dk, o_dv,
    q_c, k_c, v_c, g_c, kt_c, kt_p, kv, qg, send_kv, send_qg,
    sbuf, e_p, e_c, d_p, d_c, gp, qp, gc, qc, stat, dqt,
    st_sib, r_sib, st_own, r_chip, outs, ret,
    in_sem, s1, r1, s2, r2, s3, r3, s4, r4, s5, r5, s6, r6,
):
    p = lax.axis_index("prompt")
    g = lax.axis_index("group")
    core = lax.rem(g, 2)
    other = 1 - core
    chip = g // 2
    sibling = chip * 2 + other

    def peer_p(d):
        return lax.rem(p + d, HEADS)

    def peer_chip(d):
        return lax.rem(chip + d, CHIPS)

    def back_chip(d):
        return lax.rem(chip + CHIPS - d, CHIPS)

    def remote(src, dst, ssem, rsem, dev):
        return pltpu.make_async_remote_copy(
            src_ref=src, dst_ref=dst, send_sem=ssem, recv_sem=rsem,
            device_id=dev, device_id_type=pl.DeviceIdType.MESH,
        )

    loads = [
        pltpu.make_async_copy(src.at[0], dst, in_sem.at[i])
        for i, (src, dst) in enumerate(((cq, q_c), (ck, k_c), (cv, v_c), (cg, g_c)))
    ]
    for load in loads:
        load.start()

    barrier = pltpu.get_barrier_semaphore()
    for d in range(1, HEADS):
        pl.semaphore_signal(barrier, inc=1, device_id=(peer_p(d), g), device_id_type=pl.DeviceIdType.MESH)
    for d in range(1, CHIPS):
        pl.semaphore_signal(
            barrier, inc=1, device_id=(p, peer_chip(d) * 2 + core), device_id_type=pl.DeviceIdType.MESH
        )
    pl.semaphore_signal(barrier, inc=1, device_id=(p, sibling), device_id_type=pl.DeviceIdType.MESH)

    for h in range(HEADS):
        cols = slice(h * HS, (h + 1) * HS)
        send_kv[h, 0] = pk[:, cols]
        send_kv[h, 1] = pv[:, cols]
        send_qg[h, 0] = pq[:, cols]
        send_qg[h, 1] = pg[:, cols]
    kv[:, core, chip, p] = send_kv[p]
    qg[:, p] = send_qg[p]

    pl.semaphore_wait(barrier, HEADS - 1 + CHIPS)

    c1, c1q = [], []
    for d in range(1, HEADS):
        dev = (peer_p(d), g)
        c1.append(remote(send_kv.at[peer_p(d)], kv.at[:, core, chip, p], s1.at[0, d], r1.at[0, d], dev))
        c1q.append(remote(send_qg.at[peer_p(d)], qg.at[:, p], s1.at[1, d], r1.at[1, d], dev))
    for c in c1:
        c.start()
    for c in c1q:
        c.start()

    length = lens[0]
    for load in loads:
        load.wait()
    kt_c[...] = k_c[...].T

    diagonal = lax.broadcasted_iota(jnp.int32, (QB, QB), 0) <= lax.broadcasted_iota(jnp.int32, (QB, QB), 1)

    def cont_block(i):
        qs = slice(i * QB, (i + 1) * QB)
        q = q_c[qs, :]
        gr = g_c[qs, :]
        mx = jnp.full((8, QB), NEG, F)
        for j in range(i + 1):
            r = slice(j * QB, (j + 1) * QB)
            s = nt(k_c[r, :], q)
            if j == i:
                s = jnp.where(diagonal, s, NEG)
            sbuf[r, :] = s
            mx = jnp.maximum(mx, fold(s, jnp.max))
        m = rowmax(mx) * SCALE2
        l = jnp.zeros((8, QB), F)
        w = jnp.zeros((8, QB), F)
        for j in range(i + 1):
            r = slice(j * QB, (j + 1) * QB)
            e = jnp.exp2(sbuf[r, :] * SCALE2 - m)
            e_c[r, qs] = e.astype(B)
            dp = nt(v_c[r, :], gr).astype(B)
            d_c[r, qs] = dp
            l = l + fold(e, jnp.sum)
            w = w + fold(e * dp.astype(F), jnp.sum)
        stat[i, 0:1, :] = m
        stat[i, 1:2, :] = rowsum(l)
        stat[i, 2:3, :] = rowsum(w)

    for i in range(5):
        cont_block(i)

    for c in c1:
        c.wait()

    def block(which_core, which_chip):
        return kv.at[:, which_core, which_chip]

    c2 = [
        remote(block(core, chip), block(core, chip), s2.at[d], r2.at[d], (p, peer_chip(d) * 2 + core))
        for d in range(1, CHIPS)
    ]
    for c in c2:
        c.start()
    c3 = [remote(block(core, chip), block(core, chip), s3.at[0], r3.at[0], (p, sibling))]
    c3[0].start()

    for i in range(5, NB):
        cont_block(i)

    for d in range(1, CHIPS):
        c2[d - 1].wait_recv()
        at = block(core, back_chip(d))
        c = remote(at, at, s3.at[d], r3.at[d], (p, sibling))
        c.start()
        c3.append(c)
    for c in c1q:
        c.wait()
    for c in c3:
        c.wait_recv()

    def kv_rows(which, c):
        return kv[which, c // 4, (c % 4) * 2 : (c % 4) * 2 + 2].reshape(QB, HS)

    for c in range(NP // QB):
        kt_p[:, c * QB : (c + 1) * QB] = kv_rows(0, c).T

    def prompt_part(qs, qn, q, gr, mask, m_c, l_c, w_c):
        mx = jnp.full((8, qn), NEG, F)
        for c in range(NP // QB):
            s = nt(kv_rows(0, c), q)
            if mask is not None:
                s = jnp.where(mask(c), s, NEG)
            sbuf[c * QB : (c + 1) * QB, 0:qn] = s
            mx = jnp.maximum(mx, fold(s, jnp.max))
        m = rowmax(mx) * SCALE2
        if m_c is not None:
            m = jnp.maximum(m, m_c)
        l = jnp.zeros((8, qn), F)
        w = jnp.zeros((8, qn), F)
        for c in range(NP // QB):
            r = slice(c * QB, (c + 1) * QB)
            e = jnp.exp2(sbuf[r, 0:qn] * SCALE2 - m)
            e_p[r, qs] = e.astype(B)
            dp = nt(kv_rows(1, c), gr)
            sbuf[r, 0:qn] = dp
            l = l + fold(e, jnp.sum)
            w = w + fold(e * dp, jnp.sum)
        l = rowsum(l)
        w = rowsum(w)
        alpha = None
        if m_c is not None:
            alpha = jnp.exp2(m_c - m)
            l = l + alpha * l_c
            w = w + alpha * w_c
        inv = 1.0 / l
        delta = w * inv
        acc = jnp.zeros((HS, qn), F)
        for c in range(NP // QB):
            r = slice(c * QB, (c + 1) * QB)
            ds = e_p[r, qs] * (sbuf[r, 0:qn] - delta).astype(B)
            d_p[r, qs] = ds
            acc = acc + nn(kt_p[:, r], ds)
        return acc, inv, delta, alpha

    def column(row, qn):
        return jnp.broadcast_to(row, (HS, qn)).T

    q0 = qg[0].reshape(PQ, HS)
    g0 = qg[1].reshape(PQ, HS)

    def prompt_mask(c):
        row = lax.broadcasted_iota(jnp.int32, (QB, 1), 0)
        key_group = ((c % 4) * 2 + row // HS) * 2 + c // 4
        key_pos = ((row % HS) // 16) * 256 + key_group * 16 + row % 16
        col = lax.broadcasted_iota(jnp.int32, (1, PQ), 1)
        query_pos = (col // 16) * 256 + g * 16 + col % 16
        return key_pos <= query_pos

    acc, inv, _, _ = prompt_part(slice(NC, NQ), PQ, q0, g0, prompt_mask, None, None, None)
    outs[0] = (acc * (inv * SCALE)).T.astype(B).reshape(HEADS, 16, HS)
    inv_col = column(inv, PQ)
    gp[NC:NQ, :] = (g0.astype(F) * inv_col).astype(B)
    qp[NC:NQ, :] = (q0.astype(F) * (inv_col * SCALE)).astype(B)

    def member_block(i, carry):
        off = pl.multiple_of(i * QB, QB)
        qs = pl.ds(off, QB)
        q = q_c[qs, :]
        gr = g_c[qs, :]
        row = stat[i]
        acc, inv, delta, alpha = prompt_part(qs, QB, q, gr, None, row[0:1], row[1:2], row[2:3])
        live = (lax.broadcasted_iota(jnp.int32, (1, QB), 1) + off) < length
        inv = jnp.where(live, inv, 0.0)
        inv_c = inv * alpha
        stat[i, 3:4, :] = delta
        stat[i, 4:5, :] = inv_c
        dqt[i] = acc * inv
        inv_col = column(inv, QB)
        inv_c_col = column(inv_c, QB)
        qf = q.astype(F) * SCALE
        gf = gr.astype(F)
        gp[qs, :] = (gf * inv_col).astype(B)
        qp[qs, :] = (qf * inv_col).astype(B)
        gc[qs, :] = (gf * inv_c_col).astype(B)
        qc[qs, :] = (qf * inv_c_col).astype(B)
        return carry

    lax.fori_loop(0, NB, member_block, 0)

    half = NP // 4

    def parts(which_core, u):
        r = pl.ds(pl.multiple_of(which_core * (NP // 2) + u * half, half), half)
        return nn(d_p[r, :], qp[...]), nn(e_p[r, :], gp[...])

    c4 = []
    for u in range(2):
        dk, dv = parts(other, u)
        st_sib[u, 0] = dk.astype(B)
        st_sib[u, 1] = dv.astype(B)
        c = remote(st_sib.at[u], r_sib.at[u], s4.at[u], r4.at[u], (p, sibling))
        c.start()
        c4.append(c)
    for u in range(2):
        dk, dv = parts(core, u)
        c4[u].wait_recv()
        st_own[u, 0] = (dk + r_sib[u, 0].astype(F)).astype(B).reshape(4, HS, HS)
        st_own[u, 1] = (dv + r_sib[u, 1].astype(F)).astype(B).reshape(4, HS, HS)
        for k in range(4):
            to = u * 4 + k
            d = lax.rem(to + CHIPS - chip, CHIPS)

            @pl.when(d == 0)
            def _():
                r_chip[0] = st_own[u, :, k]

            @pl.when(d != 0)
            def _():
                remote(
                    st_own.at[u, :, k], r_chip.at[d], s5.at[d], r5.at[d], (p, to * 2 + core)
                ).start()

    def cont_grads(i):
        qs = slice(i * QB, (i + 1) * QB)
        delta = stat[i, 3:4, :]
        inv_c = stat[i, 4:5, :]
        acc = jnp.zeros((HS, QB), F)
        for j in range(i + 1):
            r = slice(j * QB, (j + 1) * QB)
            ds = e_c[r, qs] * (d_c[r, qs].astype(F) - delta).astype(B)
            d_c[r, qs] = ds
            acc = acc + nn(kt_c[:, r], ds)
        o_dq[0, qs, :] = ((dqt[i] + acc * inv_c) * SCALE).T.astype(B)

    for i in range(NB):
        cont_grads(i)

    def cont_key(j):
        r = slice(j * QB, (j + 1) * QB)
        qs = slice(j * QB, NC)
        o_dk[0, r, :] = nn(d_c[r, qs], qc[qs, :]).astype(B)
        o_dv[0, r, :] = nn(e_c[r, qs], gc[qs, :]).astype(B)

    for j in range(0, 3):
        cont_key(j)

    for d in range(1, CHIPS):
        remote(r_chip.at[d], r_chip.at[d], s5.at[d], r5.at[d], (p, sibling)).wait_recv()
    total = r_chip[0].astype(F)
    for d in range(1, CHIPS):
        total = total + r_chip[d].astype(F)
    outs[1:3] = total.astype(B).reshape(2, HEADS, 16, HS)

    c6 = []
    for d in range(1, HEADS):
        c = remote(outs.at[:, peer_p(d)], ret.at[:, p], s6.at[d], r6.at[d], (peer_p(d), g))
        c.start()
        c6.append(c)
    ret[:, p] = outs[:, p]

    for j in range(3, NB):
        cont_key(j)

    for c in c6:
        c.wait_recv()
    for h in range(HEADS):
        cols = slice(h * HS, (h + 1) * HS)
        o_pdq[:, cols] = ret[0, h]
        o_pdk[:, cols] = ret[1, h]
        o_pdv[:, cols] = ret[2, h]

    for c in c2:
        c.wait_send()
    for c in c3:
        c.wait_send()
    for c in c4:
        c.wait_send()
    for d in range(1, CHIPS):
        remote(r_chip.at[d], r_chip.at[d], s5.at[d], r5.at[d], (p, sibling)).wait_send()
    for c in c6:
        c.wait_send()


def shards(prompt_q, prompt_k, prompt_v, prompt_grad, cont_q, cont_k, cont_v, cont_grad, lengths):
    vm = pl.BlockSpec(memory_space=pltpu.VMEM)
    anym = pl.BlockSpec(memory_space=pl.ANY)
    sm = pl.BlockSpec(memory_space=pltpu.SMEM)
    small = jax.ShapeDtypeStruct((16, HEADS * HS), B)
    large = jax.ShapeDtypeStruct((1, NC, HS), B)
    dma = pltpu.SemaphoreType.DMA
    vmem = pltpu.VMEM
    return pl.pallas_call(
        kernel,
        out_shape=[small] * 3 + [large] * 3,
        in_specs=[vm] * 4 + [anym] * 4 + [sm],
        out_specs=[vm] * 6,
        scratch_shapes=[vmem((NC, HS), B)] * 4
        + [
            vmem((HS, NC), B),
            vmem((HS, NP), B),
            vmem((2, 2, CHIPS, HEADS, 16, HS), B),
            vmem((2, HEADS, 16, HS), B),
            vmem((HEADS, 2, 16, HS), B),
            vmem((HEADS, 2, 16, HS), B),
            vmem((NP, QB), F),
            vmem((NP, NQ), B),
            vmem((NC, NC), B),
            vmem((NP, NQ), B),
            vmem((NC, NC), B),
            vmem((NQ, HS), B),
            vmem((NQ, HS), B),
            vmem((NC, HS), B),
            vmem((NC, HS), B),
            vmem((NB, 8, QB), F),
            vmem((NB, HS, QB), F),
            vmem((2, 2, NP // 4, HS), B),
            vmem((2, 2, NP // 4, HS), B),
            vmem((2, 2, 4, HS, HS), B),
            vmem((CHIPS, 2, HS, HS), B),
            vmem((3, HEADS, 16, HS), B),
            vmem((3, HEADS, 16, HS), B),
            dma((4,)),
            dma((2, HEADS)),
            dma((2, HEADS)),
        ]
        + [dma((CHIPS,))] * 4
        + [dma((2,))] * 2
        + [dma((CHIPS,))] * 2
        + [dma((HEADS,))] * 2,
        compiler_params=pltpu.CompilerParams(
            collective_id=0, has_side_effects=True, vmem_limit_bytes=60 * 2**20
        ),
    )(prompt_q, prompt_k, prompt_v, prompt_grad, cont_q, cont_k, cont_v, cont_grad, lengths)


def solution(mesh):
    rows = P(("prompt", "group"), None)
    member = P("group", None, "prompt")
    return jax.shard_map(
        shards,
        mesh=mesh,
        in_specs=(rows,) * 4 + (member,) * 4 + (P("group"),),
        out_specs=(rows,) * 3 + (member,) * 3,
        check_vma=False,
    )
```

time: 325 us -> 65.9 us (0.20)
  the two profiles are of different devices: /device:TPU:1 before, /device:TPU:6 now
where the time goes in v1:
time: 65.9 us; the launch traced here: 65.5 us
  Pallas kernels  57.5 us (87%)
  local copies, waits for them, and re-layouts  6.72 us (10%)
  between operations  1.3 us (2%)
    pallas_call x1, Pallas kernels, shards(): pl.pallas_call(kernel, out_shape=[small] * 3 + [large] * 3, in_specs=[vm]...  57.5 us
    unnamed x14, local copies, waits for them, and re-layouts  6.72 us

profile of v1, /device:TPU:6, one launch (start us, length us, event | category | flops | bytes accessed | tf_op | source)
XLA Modules:
  0.0 65.5 jit_solution(5197613254923438502)
XLA Ops:
  1.3 57.5 %shard_map.136 = (bf16[16,1024]{1,0:T(8,128)(2,1)}, bf16[16,1024]{1,0:T(8,128)(2,1)}, bf16[16,1024]{1,0:T(8,128)(2,1)}, bf16[1,2048,128]{2,1,0:T(8,128)(2,1)}, b...) custom-call(bf16[16,1024]{1,0:T(8,128)(2,1)} %pq.1, bf16[16,1024]{1,0:T(8,128)(2,1)} %pk.1, ...), custom_call_target="tpu_custom_call" | custom-call | tf_op jit(solution)/shard_map/pallas_call | solution.py:371
  58.8 0.0 copy-start.3
  58.8 1.4 %copy.22 = bf16[16,1024]{1,0:T(8,128)(2,1)} copy(bf16[16,1024]{1,0:T(8,128)(2,1)} %get-tuple-element.12) | data formatting | bytes 65536
  60.2 0.0 copy-done.3
  60.2 0.0 copy-start.2
  60.2 0.6 copy.23
  60.8 0.2 copy-done.2
  61.0 0.6 copy.24
  61.6 0.0 copy-start.1
  61.6 1.9 %copy.25 = bf16[1,2048,128]{2,1,0:T(8,128)(2,1)} copy(bf16[1,2048,128]{2,1,0:T(8,128)(2,1)} %get-tuple-element.15) | data formatting | bytes 1048576
  63.5 0.0 copy-done.1
  63.5 0.0 copy-start
  63.5 0.8 %copy.26 = bf16[1,2048,128]{2,1,0:T(8,128)(2,1)} copy(bf16[1,2048,128]{2,1,0:T(8,128)(2,1)S(1)} %copy-done.1) | data formatting | bytes 1048576
  64.3 0.4 copy-done
  64.7 0.8 %copy.27 = bf16[1,2048,128]{2,1,0:T(8,128)(2,1)} copy(bf16[1,2048,128]{2,1,0:T(8,128)(2,1)S(1)} %copy-done) | data formatting | bytes 1048576
Async XLA Ops:
  58.8 1.4 %copy-start.3 = (bf16[16,1024]{1,0:T(8,128)(2,1)S(1)}, bf16[16,1024]{1,0:T(8,128)(2,1)}, u32[]{:S(2)}) copy-start(bf16[16,1024]{1,0:T(8,128)(2,1)} %get-tuple-element.13) | copy-start | bytes 98308
  60.2 0.8 %copy-start.2 = (bf16[16,1024]{1,0:T(8,128)(2,1)S(1)}, bf16[16,1024]{1,0:T(8,128)(2,1)}, u32[]{:S(2)}) copy-start(bf16[16,1024]{1,0:T(8,128)(2,1)} %get-tuple-element.14) | copy-start | bytes 98308
  61.6 1.9 %copy-start.1 = (bf16[1,2048,128]{2,1,0:T(8,128)(2,1)S(1)}, bf16[1,2048,128]{2,1,0:T(8,128)(2,1)}, u32[]{:S(2)}) copy-start(bf16[1,2048,128]{2,1,0:T(8,128)(2,1)} %get-tuple-element.16) | copy-start | bytes 1572868
  63.5 1.2 %copy-start = (bf16[1,2048,128]{2,1,0:T(8,128)(2,1)S(1)}, bf16[1,2048,128]{2,1,0:T(8,128)(2,1)}, u32[]{:S(2)}) copy-start(bf16[1,2048,128]{2,1,0:T(8,128)(2,1)} %get-tuple-element.17) | copy-start | bytes 1572868

commit v2 on v1

v2 whole, which is shorter than its diff:
```python
import functools
import math

import jax
import jax.numpy as jnp
from jax import lax
from jax.experimental import pallas as pl
from jax.experimental.pallas import tpu as pltpu
from jax.sharding import PartitionSpec as P

F = jnp.float32
B = jnp.bfloat16
HS = 128
NP = 2048
NC = 2048
QB = 256
NB = NC // QB
PQ = 128
NQ = NC + PQ
HEADS = 8
CHIPS = 8
MESH = pl.DeviceIdType.MESH
SCALE = HS**-0.5
SCALE2 = SCALE * math.log2(math.e)
NEG = -1e30


def nt(a, b):
    return lax.dot_general(a, b, (((1,), (1,)), ((), ())), preferred_element_type=F)


def nn(a, b):
    return jnp.dot(a, b, preferred_element_type=F)


def fold(x, op):
    return op(x.reshape(x.shape[0] // 8, 8, x.shape[1]), axis=0)


def rowmax(x):
    return jnp.max(x, axis=0, keepdims=True)


def rowsum(x):
    return jnp.sum(x, axis=0, keepdims=True)


def kernel(
    pq, pk, pv, pg, cq, ck, cv, cg, lens,
    o_pdq, o_pdk, o_pdv, o_dq, o_dk, o_dv,
    q_c, k_c, v_c, g_c, rows_in, kt_c, kt_p, kv, qg, send_kv, send_qg,
    sbuf, e_p, e_c, d_p, d_c, gp, qp, gc, qc, stat, dqt,
    st_sib, r_sib, st_own, r_own, dq_out, dq_in,
    lens_in, in_sem, s1, r1, s2, r2, s3, r3, s4, r4, s5, r5, s6, r6,
):
    p = lax.axis_index("prompt")
    g = lax.axis_index("group")
    core = lax.rem(g, 2)
    other = 1 - core
    chip = g // 2
    sibling = chip * 2 + other

    def peer_p(d):
        return lax.rem(p + d, HEADS)

    def peer_chip(d):
        return lax.rem(chip + d, CHIPS)

    def back_chip(d):
        return lax.rem(chip + CHIPS - d, CHIPS)

    def remote(src, dst, ssem, rsem, dev):
        return pltpu.make_async_remote_copy(
            src_ref=src, dst_ref=dst, send_sem=ssem, recv_sem=rsem, device_id=dev, device_id_type=MESH
        )

    barrier = pltpu.get_barrier_semaphore()
    for dc in range(CHIPS):
        for dp in range(HEADS):
            if dc or dp:
                pl.semaphore_signal(
                    barrier, inc=1, device_id=(peer_p(dp), peer_chip(dc) * 2 + core), device_id_type=MESH
                )
    pl.semaphore_signal(barrier, inc=1, device_id=(p, sibling), device_id_type=MESH)

    loads = [
        pltpu.make_async_copy(src, dst, in_sem.at[i])
        for i, (src, dst) in enumerate(
            (
                (ck.at[0], k_c), (cq.at[0], q_c), (cv.at[0], v_c), (cg.at[0], g_c),
                (pk, rows_in.at[0]), (pv, rows_in.at[1]), (pq, rows_in.at[2]), (pg, rows_in.at[3]),
                (lens, lens_in),
            )
        )
    ]
    for load in loads:
        load.start()
    for load in loads:
        load.wait()
    length = lens_in[0]

    for h in range(HEADS):
        cols = slice(h * HS, (h + 1) * HS)
        send_kv[h, 0] = rows_in[0, :, cols]
        send_kv[h, 1] = rows_in[1, :, cols]
        send_qg[h, 0] = rows_in[2, :, cols]
        send_qg[h, 1] = rows_in[3, :, cols]
    kv[0, chip, p] = send_kv[p]
    qg[p] = send_qg[p]

    diagonal = lax.broadcasted_iota(jnp.int32, (QB, QB), 0) <= lax.broadcasted_iota(jnp.int32, (QB, QB), 1)

    def cont_block(i):
        qs = slice(i * QB, (i + 1) * QB)
        q = q_c[qs, :]
        gr = g_c[qs, :]
        mx = jnp.full((8, QB), NEG, F)
        for j in range(i + 1):
            r = slice(j * QB, (j + 1) * QB)
            s = nt(k_c[r, :], q)
            if j == i:
                s = jnp.where(diagonal, s, NEG)
            sbuf[r, :] = s
            mx = jnp.maximum(mx, fold(s, jnp.max))
        m = rowmax(mx) * SCALE2
        l = jnp.zeros((8, QB), F)
        w = jnp.zeros((8, QB), F)
        for j in range(i + 1):
            r = slice(j * QB, (j + 1) * QB)
            e = jnp.exp2(sbuf[r, :] * SCALE2 - m)
            e_c[r, qs] = e.astype(B)
            dp = nt(v_c[r, :], gr).astype(B)
            d_c[r, qs] = dp
            l = l + fold(e, jnp.sum)
            w = w + fold(e * dp.astype(F), jnp.sum)
        stat[i, 0:1, :] = m
        stat[i, 1:2, :] = rowsum(l)
        stat[i, 2:3, :] = rowsum(w)

    for i in range(NB):
        cont_block(i)

    pl.semaphore_wait(barrier, HEADS * CHIPS)

    for dc in range(CHIPS):
        for dp in range(HEADS):
            if dc or dp:
                remote(
                    send_kv.at[peer_p(dp)], kv.at[0, chip, p], s1.at[dc], r1.at[dc],
                    (peer_p(dp), peer_chip(dc) * 2 + core),
                ).start()
        if dc == 0:
            for dp in range(1, HEADS):
                remote(send_qg.at[peer_p(dp)], qg.at[p], s2.at[0], r2.at[0], (peer_p(dp), g)).start()

    kt_c[...] = k_c[...].T

    forwards = []
    for dc in range(CHIPS):
        at = kv.at[0, back_chip(dc)]
        whole = at if dc else kv.at[0, back_chip(dc), 0 : HEADS - 1]
        remote(whole, whole, s1.at[dc], r1.at[dc], (p, sibling)).wait()
        c = remote(at, kv.at[1, back_chip(dc)], s3.at[dc], r3.at[dc], (p, sibling))
        c.start()
        forwards.append(c)
    seven = qg.at[0 : HEADS - 1]
    remote(seven, seven, s2.at[0], r2.at[0], (p, sibling)).wait()

    def kv_rows(which, c):
        return kv[c // 4, (c % 4) * 2 : (c % 4) * 2 + 2, :, which].reshape(QB, HS)

    for c in range(NP // QB):
        if c == 4:
            for f in forwards:
                f.wait_recv()
        kt_p[:, c * QB : (c + 1) * QB] = kv_rows(0, c).T

    def prompt_part(qs, qn, q, gr, mask, m_c, l_c, w_c):
        mx = jnp.full((8, qn), NEG, F)
        for c in range(NP // QB):
            s = nt(kv_rows(0, c), q)
            if mask is not None:
                s = jnp.where(mask(c), s, NEG)
            sbuf[c * QB : (c + 1) * QB, 0:qn] = s
            mx = jnp.maximum(mx, fold(s, jnp.max))
        m = rowmax(mx) * SCALE2
        if m_c is not None:
            m = jnp.maximum(m, m_c)
        l = jnp.zeros((8, qn), F)
        w = jnp.zeros((8, qn), F)
        for c in range(NP // QB):
            r = slice(c * QB, (c + 1) * QB)
            e = jnp.exp2(sbuf[r, 0:qn] * SCALE2 - m)
            e_p[r, qs] = e.astype(B)
            dp = nt(kv_rows(1, c), gr)
            sbuf[r, 0:qn] = dp
            l = l + fold(e, jnp.sum)
            w = w + fold(e * dp, jnp.sum)
        l = rowsum(l)
        w = rowsum(w)
        alpha = None
        if m_c is not None:
            alpha = jnp.exp2(m_c - m)
            l = l + alpha * l_c
            w = w + alpha * w_c
        inv = 1.0 / l
        delta = w * inv
        acc = jnp.zeros((HS, qn), F)
        for c in range(NP // QB):
            r = slice(c * QB, (c + 1) * QB)
            ds = e_p[r, qs] * (sbuf[r, 0:qn] - delta).astype(B)
            d_p[r, qs] = ds
            acc = acc + nn(kt_p[:, r], ds)
        return acc, inv, delta, alpha

    def column(row, qn):
        return jnp.broadcast_to(row, (HS, qn)).T

    q0 = qg[:, 0].reshape(PQ, HS)
    g0 = qg[:, 1].reshape(PQ, HS)

    def prompt_mask(c):
        row = lax.broadcasted_iota(jnp.int32, (QB, 1), 0)
        key_core = core if c < 4 else other
        key_group = ((c % 4) * 2 + row // HS) * 2 + key_core
        key_pos = ((row % HS) // 16) * 256 + key_group * 16 + row % 16
        col = lax.broadcasted_iota(jnp.int32, (1, PQ), 1)
        query_pos = (col // 16) * 256 + g * 16 + col % 16
        return key_pos <= query_pos

    acc, inv, _, _ = prompt_part(slice(NC, NQ), PQ, q0, g0, prompt_mask, None, None, None)
    dq_out[...] = (acc * (inv * SCALE)).T.astype(B).reshape(HEADS, 16, HS)
    for dp in range(1, HEADS):
        remote(dq_out.at[peer_p(dp)], dq_in.at[p], s6.at[0], r6.at[0], (peer_p(dp), g)).start()
    dq_in[p] = dq_out[p]
    inv_col = column(inv, PQ)
    gp[NC:NQ, :] = (g0.astype(F) * inv_col).astype(B)
    qp[NC:NQ, :] = (q0.astype(F) * (inv_col * SCALE)).astype(B)

    def member_block(i, carry):
        off = pl.multiple_of(i * QB, QB)
        qs = pl.ds(off, QB)
        q = q_c[qs, :]
        gr = g_c[qs, :]
        row = stat[i]
        acc, inv, delta, alpha = prompt_part(qs, QB, q, gr, None, row[0:1], row[1:2], row[2:3])
        live = (lax.broadcasted_iota(jnp.int32, (1, QB), 1) + off) < length
        inv = jnp.where(live, inv, 0.0)
        inv_c = inv * alpha
        stat[i, 3:4, :] = delta
        stat[i, 4:5, :] = inv_c
        dqt[i] = acc * inv
        inv_col = column(inv, QB)
        inv_c_col = column(inv_c, QB)
        qf = q.astype(F) * SCALE
        gf = gr.astype(F)
        gp[qs, :] = (gf * inv_col).astype(B)
        qp[qs, :] = (qf * inv_col).astype(B)
        gc[qs, :] = (gf * inv_c_col).astype(B)
        qc[qs, :] = (qf * inv_c_col).astype(B)
        return carry

    lax.fori_loop(0, NB, member_block, 0)

    half = NP // 4

    def parts(which, u):
        r = slice(which * (NP // 2) + u * half, which * (NP // 2) + (u + 1) * half)
        return nn(d_p[r, :], qp[...]), nn(e_p[r, :], gp[...])

    to_sibling = []
    for u in range(2):
        dk, dv = parts(1, u)
        st_sib[u, 0] = dk.astype(B)
        st_sib[u, 1] = dv.astype(B)
        c = remote(st_sib.at[u], r_sib.at[u], s4.at[u], r4.at[u], (p, sibling))
        c.start()
        to_sibling.append(c)
    slot = p * CHIPS + chip
    for u in range(2):
        dk, dv = parts(0, u)
        to_sibling[u].wait_recv()
        st_own[u * 4 : u * 4 + 4, :, 0] = (dk + r_sib[u, 0].astype(F)).astype(B).reshape(4, HEADS, 16, HS)
        st_own[u * 4 : u * 4 + 4, :, 1] = (dv + r_sib[u, 1].astype(F)).astype(B).reshape(4, HEADS, 16, HS)
        for k in range(4):
            to = u * 4 + k
            for dp in range(1, HEADS):
                remote(
                    st_own.at[to, peer_p(dp)], r_own.at[slot], s5.at[0], r5.at[0],
                    (peer_p(dp), to * 2 + core),
                ).start()

            @pl.when(chip != to)
            def _():
                remote(
                    st_own.at[to, p], r_own.at[slot], s5.at[0], r5.at[0], (p, to * 2 + core)
                ).start()

    r_own[slot] = st_own[chip, p]

    def cont_grads(i):
        qs = slice(i * QB, (i + 1) * QB)
        delta = stat[i, 3:4, :]
        inv_c = stat[i, 4:5, :]
        acc = jnp.zeros((HS, QB), F)
        for j in range(i + 1):
            r = slice(j * QB, (j + 1) * QB)
            ds = e_c[r, qs] * (d_c[r, qs].astype(F) - delta).astype(B)
            d_c[r, qs] = ds
            acc = acc + nn(kt_c[:, r], ds)
        o_dq[0, qs, :] = ((dqt[i] + acc * inv_c) * SCALE).T.astype(B)

    for i in range(NB):
        cont_grads(i)

    def cont_key(j):
        r = slice(j * QB, (j + 1) * QB)
        qs = slice(j * QB, NC)
        o_dk[0, r, :] = nn(d_c[r, qs], qc[qs, :]).astype(B)
        o_dv[0, r, :] = nn(e_c[r, qs], gc[qs, :]).astype(B)

    for j in range(NB):
        cont_key(j)

    seven = dq_in.at[0 : HEADS - 1]
    remote(seven, seven, s6.at[0], r6.at[0], (p, sibling)).wait()
    for h in range(HEADS):
        o_pdq[:, h * HS : (h + 1) * HS] = dq_in[h]

    arrived = r_own.at[0 : HEADS * CHIPS - 1]
    remote(arrived, arrived, s5.at[0], r5.at[0], (p, sibling)).wait()
    for h in range(HEADS):
        cols = slice(h * HS, (h + 1) * HS)
        total = jnp.sum(r_own[h * CHIPS : (h + 1) * CHIPS].astype(F), axis=0)
        o_pdk[:, cols] = total[0].astype(B)
        o_pdv[:, cols] = total[1].astype(B)

    for c in forwards:
        c.wait_send()
    for c in to_sibling:
        c.wait_send()


def hand_over(*refs):
    ins, outs, sem = refs[:6], refs[6:12], refs[12]
    copies = [pltpu.make_async_copy(a, b, sem.at[i]) for i, (a, b) in enumerate(zip(ins, outs))]
    for c in copies:
        c.start()
    for c in copies:
        c.wait()


def shards(prompt_q, prompt_k, prompt_v, prompt_grad, cont_q, cont_k, cont_v, cont_grad, lengths):
    vm = pl.BlockSpec(memory_space=pltpu.VMEM)
    hbm = pl.BlockSpec(memory_space=pltpu.HBM)
    dma = pltpu.SemaphoreType.DMA
    vmem = pltpu.VMEM
    shapes = [(16, HEADS * HS)] * 3 + [(1, NC, HS)] * 3
    results = pl.pallas_call(
        kernel,
        out_shape=[vmem(shape, B) for shape in shapes],
        in_specs=[hbm] * 9,
        out_specs=[vm] * 6,
        scratch_shapes=[vmem((NC, HS), B)] * 4
        + [
            vmem((4, 16, HEADS * HS), B),
            vmem((HS, NC), B),
            vmem((HS, NP), B),
            vmem((2, CHIPS, HEADS, 2, 16, HS), B),
            vmem((HEADS, 2, 16, HS), B),
            vmem((HEADS, 2, 16, HS), B),
            vmem((HEADS, 2, 16, HS), B),
            vmem((NP, QB), F),
            vmem((NP, NQ), B),
            vmem((NC, NC), B),
            vmem((NP, NQ), B),
            vmem((NC, NC), B),
            vmem((NQ, HS), B),
            vmem((NQ, HS), B),
            vmem((NC, HS), B),
            vmem((NC, HS), B),
            vmem((NB, 8, QB), F),
            vmem((NB, HS, QB), F),
            vmem((2, 2, NP // 4, HS), B),
            vmem((2, 2, NP // 4, HS), B),
            vmem((CHIPS, HEADS, 2, 16, HS), B),
            vmem((HEADS * CHIPS, 2, 16, HS), B),
            vmem((HEADS, 16, HS), B),
            vmem((HEADS, 16, HS), B),
            pltpu.SMEM((1,), jnp.int32),
            dma((9,)),
            dma((CHIPS,)),
            dma((CHIPS,)),
            dma((1,)),
            dma((1,)),
            dma((CHIPS,)),
            dma((CHIPS,)),
            dma((2,)),
            dma((2,)),
        ]
        + [dma((1,))] * 4,
        compiler_params=pltpu.CompilerParams(
            collective_id=0, has_side_effects=True, vmem_limit_bytes=54 * 2**20
        ),
    )(prompt_q, prompt_k, prompt_v, prompt_grad, cont_q, cont_k, cont_v, cont_grad, lengths)
    return pl.pallas_call(
        hand_over,
        out_shape=[jax.ShapeDtypeStruct(shape, B) for shape in shapes],
        in_specs=[vm] * 6,
        out_specs=[hbm] * 6,
        scratch_shapes=[dma((6,))],
    )(*[pltpu.with_memory_space_constraint(x, pltpu.VMEM) for x in results])


def solution(mesh):
    rows = P(("prompt", "group"), None)
    member = P("group", None, "prompt")
    return jax.shard_map(
        shards,
        mesh=mesh,
        in_specs=(rows,) * 4 + (member,) * 4 + (P("group"),),
        out_specs=(rows,) * 3 + (member,) * 3,
        check_vma=False,
    )
```

time: 65.9 us -> 54.8 us (0.83)
  the two profiles are of different devices: /device:TPU:6 before, /device:TPU:1 now
where the time goes in v2:
time: 54.8 us; the launch traced here: 54.3 us
  Pallas kernels  52.9 us (97%)
  between operations  1.45 us (3%)
    pallas_call x1, Pallas kernels, shards(): pl.pallas_call(kernel, out_shape=[vmem(shape, B) for shape in shapes], in...  51.6 us
    pallas_call x1, Pallas kernels, shards(): pl.pallas_call(hand_over, out_shape=[jax.ShapeDtypeStruct(shape, B) for s...  1.23 us

profile of v2, /device:TPU:1, one launch (start us, length us, event | category | flops | bytes accessed | tf_op | source)
XLA Modules:
  0.0 54.3 jit_solution(18329694447987356117)
XLA Ops:
  1.3 51.6 %shard_map.136 = (bf16[16,1024]{1,0:T(8,128)(2,1)S(1)}, bf16[16,1024]{1,0:T(8,128)(2,1)S(1)}, bf16[16,1024]{1,0:T(8,128)(2,1)S(1)}, bf16[1,2048,128]{2,1,0:T(8,1...) custom-call(bf16[16,1024]{1,0:T(8,128)(2,1)} %pq.1, bf16[16,1024]{1,0:T(8,128)(2,1)} %pk.1, ...), custom_call_target="tpu_custom_call" | custom-call | tf_op jit(solution)/shard_map/pallas_call | solution.py:359
  52.9 1.2 %shard_map.137 = (bf16[16,1024]{1,0:T(8,128)(2,1)}, bf16[16,1024]{1,0:T(8,128)(2,1)}, bf16[16,1024]{1,0:T(8,128)(2,1)}, bf16[1,2048,128]{2,1,0:T(8,128)(2,1)}, b...) custom-call(bf16[16,1024]{1,0:T(8,128)(2,1)S(1)} %get-tuple-element.12.refs_0_, ...), custom_call_target="tpu_custom_call" | custom-call | tf_op jit(solution)/shard_map/pallas_call | solution.py:406

commit v3 on v2

v3 whole, which is shorter than its diff:
```python
import functools
import math

import jax
import jax.numpy as jnp
from jax import lax
from jax.experimental import pallas as pl
from jax.experimental.pallas import tpu as pltpu
from jax.sharding import PartitionSpec as P

F = jnp.float32
B = jnp.bfloat16
HS = 128
NP = 2048
NC = 2048
CB = 256
QB = 512
WB = 1024
GK = NP // 2
PQ = 128
NQ = NC + PQ
HEADS = 8
CHIPS = 8
MESH = pl.DeviceIdType.MESH
SCALE = HS**-0.5
SCALE2 = SCALE * math.log2(math.e)
NEG = -1e30


def nt(a, b):
    return lax.dot_general(a, b, (((1,), (1,)), ((), ())), preferred_element_type=F)


def nn(a, b):
    return jnp.dot(a, b, preferred_element_type=F)


def fold(x, op):
    return op(x.reshape(x.shape[0] // 8, 8, x.shape[1]), axis=0)


def rowmax(x):
    return jnp.max(x, axis=0, keepdims=True)


def rowsum(x):
    return jnp.sum(x, axis=0, keepdims=True)


def kernel(
    pq, pk, pv, pg, cq, ck, cv, cg, lens,
    o_pdq, o_pdk, o_pdv, o_dq, o_dk, o_dv,
    q_all, k_c, v_c, g_all, rows_in, kt_c, kt_p, kv, qg, send_kv, send_qg,
    sbuf, e_p, e_c, d_p, d_c, stat,
    st_sib, r_sib, st_own, r_own, dq_out, dq_in,
    lens_in, in_sem, s1, r1, s2, r2, s3, r3, s4, r4, s5, r5, s6, r6,
):
    p = lax.axis_index("prompt")
    g = lax.axis_index("group")
    core = lax.rem(g, 2)
    other = 1 - core
    chip = g // 2
    sibling = chip * 2 + other

    def peer_p(d):
        return lax.rem(p + d, HEADS)

    def peer_chip(d):
        return lax.rem(chip + d, CHIPS)

    def back_chip(d):
        return lax.rem(chip + CHIPS - d, CHIPS)

    def remote(src, dst, ssem, rsem, dev):
        return pltpu.make_async_remote_copy(
            src_ref=src, dst_ref=dst, send_sem=ssem, recv_sem=rsem, device_id=dev, device_id_type=MESH
        )

    loads = [
        pltpu.make_async_copy(src, dst, in_sem.at[i])
        for i, (src, dst) in enumerate(
            (
                (pk, rows_in.at[0]), (pv, rows_in.at[1]), (pq, rows_in.at[2]), (pg, rows_in.at[3]),
                (ck.at[0], k_c), (cq.at[0], q_all.at[0:NC]), (cv.at[0], v_c), (cg.at[0], g_all.at[0:NC]),
                (lens, lens_in),
            )
        )
    ]
    for load in loads:
        load.start()

    barrier = pltpu.get_barrier_semaphore()
    for dc in range(CHIPS):
        for dp in range(HEADS):
            if dc or dp:
                pl.semaphore_signal(
                    barrier, inc=1, device_id=(peer_p(dp), peer_chip(dc) * 2 + core), device_id_type=MESH
                )
    pl.semaphore_signal(barrier, inc=1, device_id=(p, sibling), device_id_type=MESH)

    for load in loads[:4]:
        load.wait()
    for h in range(HEADS):
        cols = slice(h * HS, (h + 1) * HS)
        send_kv[h, 0] = rows_in[0, :, cols]
        send_kv[h, 1] = rows_in[1, :, cols]
        send_qg[h, 0] = rows_in[2, :, cols]
        send_qg[h, 1] = rows_in[3, :, cols]
    kv[0, 0, p] = send_kv[p]
    qg[p] = send_qg[p]

    pl.semaphore_wait(barrier, HEADS * CHIPS)

    for dc in range(CHIPS):
        for dp in range(HEADS):
            if dc or dp:
                remote(
                    send_kv.at[peer_p(dp)], kv.at[0, dc, p], s1.at[dc], r1.at[dc],
                    (peer_p(dp), peer_chip(dc) * 2 + core),
                ).start()
    for dp in range(1, HEADS):
        remote(send_qg.at[peer_p(dp)], qg.at[p], s2.at[0], r2.at[0], (peer_p(dp), g)).start()

    for load in loads[4:]:
        load.wait()
    length = lens_in[0]

    def scores(keys, values, q, gr, mask, e_ref, d_ref, rows, qs, qn):
        mx = jnp.full((8, qn), NEG, F)
        for c, r in enumerate(rows):
            s = nt(keys(c), q)
            keep = mask(c)
            if keep is not None:
                s = jnp.where(keep, s, NEG)
            sbuf[c % 4 * CB : c % 4 * CB + CB, c // 4 * qn : c // 4 * qn + qn] = s
            mx = jnp.maximum(mx, fold(s, jnp.max))
        m = rowmax(mx) * SCALE2
        l = jnp.zeros((8, qn), F)
        w = jnp.zeros((8, qn), F)
        for c, r in enumerate(rows):
            e = jnp.exp2(sbuf[c % 4 * CB : c % 4 * CB + CB, c // 4 * qn : c // 4 * qn + qn] * SCALE2 - m)
            e_ref[r, qs] = e.astype(B)
            dp = nt(values(c), gr).astype(B)
            d_ref[r, qs] = dp
            l = l + fold(e, jnp.sum)
            w = w + fold(e * dp.astype(F), jnp.sum)
        return m, rowsum(l), rowsum(w)

    def grads(rows, qs, factor, delta, e_ref, d_ref):
        low = factor.astype(B)
        for r in rows:
            probs = e_ref[r, qs] * low
            e_ref[r, qs] = probs
            d_ref[r, qs] = probs * (d_ref[r, qs].astype(F) - delta).astype(B)

    diagonal = lax.broadcasted_iota(jnp.int32, (CB, CB), 0) <= lax.broadcasted_iota(jnp.int32, (CB, CB), 1)

    def cont_rows(i):
        return [slice(j * CB, (j + 1) * CB) for j in range(i + 1)]

    def cont_scores(i):
        rows = cont_rows(i)
        qs = rows[i]
        m, l, w = scores(
            lambda c: k_c[rows[c], :], lambda c: v_c[rows[c], :], q_all[qs, :], g_all[qs, :],
            lambda c: diagonal if c == i else None, e_c, d_c, rows, qs, CB,
        )
        stat[0, 0:1, qs] = m
        stat[0, 1:2, qs] = l
        stat[0, 2:3, qs] = w

    for i in range(NC // CB):
        cont_scores(i)

    forwards = []

    def forward(dc):
        at = kv.at[0, dc]
        whole = at if dc else kv.at[0, 0, 0 : HEADS - 1]
        remote(whole, whole, s1.at[dc], r1.at[dc], (p, sibling)).wait()
        c = remote(at, kv.at[1, dc], s3.at[dc], r3.at[dc], (p, sibling))
        c.start()
        forwards.append(c)

    def kv_rows(which, r):
        first = r.start // HS
        return kv[first // CHIPS, first % CHIPS : first % CHIPS + CB // HS, :, which].reshape(CB, HS)

    groups = {1: (0, GK // 2), 2: (GK // 2, GK), 3: (GK, NP)}
    own_rows = slice(NC, NQ)

    def group_rows(k):
        return [slice(r, r + CB) for r in range(groups[k][0], groups[k][1], CB)]

    def prompt_scores(k, qs, qn, mask):
        rows = group_rows(k)
        m, l, w = scores(
            lambda c: kv_rows(0, rows[c]), lambda c: kv_rows(1, rows[c]), q_all[qs, :], g_all[qs, :],
            lambda c: mask(rows[c]), e_p, d_p, rows, qs, qn,
        )
        stat[k, 0:1, qs] = m
        stat[k, 1:2, qs] = l
        stat[k, 2:3, qs] = w

    def member_scores(k):
        def body(i, carry):
            prompt_scores(k, pl.ds(pl.multiple_of(i * WB, WB), WB), WB, lambda r: None)
            return carry

        lax.fori_loop(0, NC // WB, body, 0)

    def prompt_mask(r):
        row = lax.broadcasted_iota(jnp.int32, (CB, 1), 0)
        key_chip = chip + CHIPS - (r.start % GK // HS + row // HS)
        key_chip = jnp.where(key_chip >= CHIPS, key_chip - CHIPS, key_chip)
        key_group = key_chip * 2 + (other if r.start >= GK else core)
        key_pos = ((row % HS) // 16) * 256 + key_group * 16 + row % 16
        col = lax.broadcasted_iota(jnp.int32, (1, PQ), 1)
        query_pos = (col // 16) * 256 + g * 16 + col % 16
        return key_pos <= query_pos

    for dc in range(CHIPS // 2):
        forward(dc)
    member_scores(1)
    for dc in range(CHIPS // 2, CHIPS):
        forward(dc)
    member_scores(2)
    seven = qg.at[0 : HEADS - 1]
    remote(seven, seven, s2.at[0], r2.at[0], (p, sibling)).wait()
    q_all[own_rows, :] = qg[:, 0].reshape(PQ, HS)
    g_all[own_rows, :] = qg[:, 1].reshape(PQ, HS)
    prompt_scores(1, own_rows, PQ, prompt_mask)
    prompt_scores(2, own_rows, PQ, prompt_mask)
    for f in forwards:
        f.wait_recv()
    member_scores(3)
    prompt_scores(3, own_rows, PQ, prompt_mask)

    stat[0, 0:1, own_rows] = jnp.full((1, PQ), NEG, F)
    stat[0, 1:3, own_rows] = jnp.zeros((2, PQ), F)
    for i in range(NQ // PQ):
        qs = slice(i * PQ, (i + 1) * PQ)
        ms = [stat[k, 0:1, qs] for k in range(4)]
        top = jnp.maximum(jnp.maximum(ms[0], ms[1]), jnp.maximum(ms[2], ms[3]))
        scale = [jnp.exp2(m - top) for m in ms]
        l = sum(scale[k] * stat[k, 1:2, qs] for k in range(4))
        w = sum(scale[k] * stat[k, 2:3, qs] for k in range(4))
        inv = 1.0 / l
        delta = w * inv
        if i < NC // PQ:
            live = (lax.broadcasted_iota(jnp.int32, (1, PQ), 1) + i * PQ) < length
            inv = jnp.where(live, inv, 0.0)
        for k in range(4):
            stat[k, 3:4, qs] = scale[k] * inv
        stat[0, 4:5, qs] = delta

    def prompt_grads(k):
        def body(i, carry):
            qs = pl.ds(pl.multiple_of(i * WB, WB), WB)
            grads(group_rows(k), qs, stat[k, 3:4, qs], stat[0, 4:5, qs], e_p, d_p)
            return carry

        lax.fori_loop(0, NC // WB, body, 0)
        grads(group_rows(k), own_rows, stat[k, 3:4, own_rows], stat[0, 4:5, own_rows], e_p, d_p)

    def parts(start, size):
        r = slice(start, start + size)
        return nn(d_p[r, :], q_all[...]) * SCALE, nn(e_p[r, :], g_all[...])

    units = 4
    unit = GK // units
    prompt_grads(3)
    to_sibling = []
    for u in range(units):
        dk, dv = parts(GK + u * unit, unit)
        st_sib[u, 0] = dk.astype(B)
        st_sib[u, 1] = dv.astype(B)
        c = remote(st_sib.at[u], r_sib.at[u], s4.at[u], r4.at[u], (p, sibling))
        c.start()
        to_sibling.append(c)
    prompt_grads(1)
    prompt_grads(2)
    slot = p * CHIPS + chip
    per = CHIPS // units
    for u in range(units):
        dk, dv = parts(u * unit, unit)
        to_sibling[u].wait_recv()
        at = slice(u * per, (u + 1) * per)
        st_own[at, :, 0] = (dk + r_sib[u, 0].astype(F)).astype(B).reshape(per, HEADS, 16, HS)
        st_own[at, :, 1] = (dv + r_sib[u, 1].astype(F)).astype(B).reshape(per, HEADS, 16, HS)
        for dc in range(u * per, (u + 1) * per):
            for dp in range(HEADS):
                if dc or dp:
                    remote(
                        st_own.at[dc, peer_p(dp)], r_own.at[slot], s5.at[0], r5.at[0],
                        (peer_p(dp), back_chip(dc) * 2 + core),
                    ).start()
    r_own[slot] = st_own[0, p]

    for start in range(0, NP, CB):
        r = slice(start, start + CB)
        kt_p[:, r] = kv_rows(0, r).T
    dq = nn(kt_p[...], d_p[:, own_rows]) * SCALE
    dq_out[...] = dq.T.astype(B).reshape(HEADS, 16, HS)
    for dp in range(1, HEADS):
        remote(dq_out.at[peer_p(dp)], dq_in.at[p], s6.at[0], r6.at[0], (peer_p(dp), g)).start()
    dq_in[p] = dq_out[p]

    kt_c[...] = k_c[...].T
    for i in range(NC // CB):
        qs = slice(i * CB, (i + 1) * CB)
        grads(cont_rows(i), qs, stat[0, 3:4, qs], stat[0, 4:5, qs], e_c, d_c)

    for i in range(NC // QB):
        qs = slice(i * QB, (i + 1) * QB)
        first = slice(i * QB, i * QB + CB)
        second = slice(i * QB + CB, (i + 1) * QB)
        dq = nn(kt_p[...], d_p[:, qs])
        if i:
            dq = dq + nn(kt_c[:, 0 : i * QB], d_c[0 : i * QB, qs])
        left = nn(kt_c[:, first], d_c[first, first])
        right = nn(kt_c[:, i * QB : (i + 1) * QB], d_c[i * QB : (i + 1) * QB, second])
        dq = (dq + jnp.concatenate([left, right], axis=1)) * SCALE
        o_dq[0, qs, :] = dq.astype(B).T

    for j in range(NC // CB):
        r = slice(j * CB, (j + 1) * CB)
        qs = slice(j * CB, NC)
        o_dk[0, r, :] = (nn(d_c[r, qs], q_all[qs, :]) * SCALE).astype(B)
        o_dv[0, r, :] = nn(e_c[r, qs], g_all[qs, :]).astype(B)

    seven = dq_in.at[0 : HEADS - 1]
    remote(seven, seven, s6.at[0], r6.at[0], (p, sibling)).wait()
    for h in range(HEADS):
        o_pdq[:, h * HS : (h + 1) * HS] = dq_in[h]

    arrived = r_own.at[0 : HEADS * CHIPS - 1]
    remote(arrived, arrived, s5.at[0], r5.at[0], (p, sibling)).wait()
    for h in range(HEADS):
        cols = slice(h * HS, (h + 1) * HS)
        total = jnp.sum(r_own[h * CHIPS : (h + 1) * CHIPS].astype(F), axis=0)
        o_pdk[:, cols] = total[0].astype(B)
        o_pdv[:, cols] = total[1].astype(B)

    for c in forwards:
        c.wait_send()
    for c in to_sibling:
        c.wait_send()


def hand_over(*refs):
    ins, outs, sem = refs[:6], refs[6:12], refs[12]
    copies = [pltpu.make_async_copy(a, b, sem.at[i]) for i, (a, b) in enumerate(zip(ins, outs))]
    for c in copies:
        c.start()
    for c in copies:
        c.wait()


def shards(prompt_q, prompt_k, prompt_v, prompt_grad, cont_q, cont_k, cont_v, cont_grad, lengths):
    vm = pl.BlockSpec(memory_space=pltpu.VMEM)
    hbm = pl.BlockSpec(memory_space=pltpu.HBM)
    dma = pltpu.SemaphoreType.DMA
    vmem = pltpu.VMEM
    shapes = [(16, HEADS * HS)] * 3 + [(1, NC, HS)] * 3
    results = pl.pallas_call(
        kernel,
        out_shape=[vmem(shape, B) for shape in shapes],
        in_specs=[hbm] * 9,
        out_specs=[vm] * 6,
        scratch_shapes=[
            vmem((NQ, HS), B),
            vmem((NC, HS), B),
            vmem((NC, HS), B),
            vmem((NQ, HS), B),
            vmem((4, 16, HEADS * HS), B),
            vmem((HS, NC), B),
            vmem((HS, NP), B),
            vmem((2, CHIPS, HEADS, 2, 16, HS), B),
            vmem((HEADS, 2, 16, HS), B),
            vmem((HEADS, 2, 16, HS), B),
            vmem((HEADS, 2, 16, HS), B),
            vmem((GK, WB), F),
            vmem((NP, NQ), B),
            vmem((NC, NC), B),
            vmem((NP, NQ), B),
            vmem((NC, NC), B),
            vmem((4, 8, NQ), F),
            vmem((4, 2, GK // 4, HS), B),
            vmem((4, 2, GK // 4, HS), B),
            vmem((CHIPS, HEADS, 2, 16, HS), B),
            vmem((HEADS * CHIPS, 2, 16, HS), B),
            vmem((HEADS, 16, HS), B),
            vmem((HEADS, 16, HS), B),
            pltpu.SMEM((1,), jnp.int32),
            dma((9,)),
            dma((CHIPS,)),
            dma((CHIPS,)),
            dma((1,)),
            dma((1,)),
            dma((CHIPS,)),
            dma((CHIPS,)),
            dma((4,)),
            dma((4,)),
        ]
        + [dma((1,))] * 4,
        compiler_params=pltpu.CompilerParams(
            collective_id=0, has_side_effects=True, vmem_limit_bytes=58 * 2**20
        ),
    )(prompt_q, prompt_k, prompt_v, prompt_grad, cont_q, cont_k, cont_v, cont_grad, lengths)
    return pl.pallas_call(
        hand_over,
        out_shape=[jax.ShapeDtypeStruct(shape, B) for shape in shapes],
        in_specs=[vm] * 6,
        out_specs=[hbm] * 6,
        scratch_shapes=[dma((6,))],
    )(*[pltpu.with_memory_space_constraint(x, pltpu.VMEM) for x in results])


def solution(mesh):
    rows = P(("prompt", "group"), None)
    member = P("group", None, "prompt")
    return jax.shard_map(
        shards,
        mesh=mesh,
        in_specs=(rows,) * 4 + (member,) * 4 + (P("group"),),
        out_specs=(rows,) * 3 + (member,) * 3,
        check_vma=False,
    )
```

time: 54.8 us -> 48.8 us (0.89)
  Pallas kernels: 52.9 us -> 47.1 us
    pallas_call x1, Pallas kernels: 51.6 us -> 45.9 us  [shards(): pl.pallas_call(kernel, out_shape=[vmem(shape, B) for shape in shapes], in...]
where the time goes in v3:
time: 48.8 us; the launch traced here: 48.6 us
  Pallas kernels  47.1 us (97%)
  between operations  1.47 us (3%)
    pallas_call x1, Pallas kernels, shards(): pl.pallas_call(kernel, out_shape=[vmem(shape, B) for shape in shapes], in...  45.9 us
    pallas_call x1, Pallas kernels, shards(): pl.pallas_call(hand_over, out_shape=[jax.ShapeDtypeStruct(shape, B) for s...  1.23 us

profile of v3, /device:TPU:1, one launch (start us, length us, event | category | flops | bytes accessed | tf_op | source)
XLA Modules:
  0.0 48.6 jit_solution(14344222317556600879)
XLA Ops:
  1.3 45.9 %shard_map.136 = (bf16[16,1024]{1,0:T(8,128)(2,1)S(1)}, bf16[16,1024]{1,0:T(8,128)(2,1)S(1)}, bf16[16,1024]{1,0:T(8,128)(2,1)S(1)}, bf16[1,2048,128]{2,1,0:T(8,1...) custom-call(bf16[16,1024]{1,0:T(8,128)(2,1)} %pq.1, bf16[16,1024]{1,0:T(8,128)(2,1)} %pk.1, ...), custom_call_target="tpu_custom_call" | custom-call | tf_op jit(solution)/shard_map/pallas_call | solution.py:366
  47.2 1.2 %shard_map.137 = (bf16[16,1024]{1,0:T(8,128)(2,1)}, bf16[16,1024]{1,0:T(8,128)(2,1)}, bf16[16,1024]{1,0:T(8,128)(2,1)}, bf16[1,2048,128]{2,1,0:T(8,128)(2,1)}, b...) custom-call(bf16[16,1024]{1,0:T(8,128)(2,1)S(1)} %get-tuple-element.12.refs_0_, ...), custom_call_target="tpu_custom_call" | custom-call | tf_op jit(solution)/shard_map/pallas_call | solution.py:411

commit v4 on v3

--- a/solution.py
+++ b/solution.py
@@ -51,7 +51,7 @@
     pq, pk, pv, pg, cq, ck, cv, cg, lens,
     o_pdq, o_pdk, o_pdv, o_dq, o_dk, o_dv,
     q_all, k_c, v_c, g_all, rows_in, kt_c, kt_p, kv, qg, send_kv, send_qg,
-    sbuf, e_p, e_c, d_p, d_c, stat,
+    q_two, sbuf, e_p, e_c, d_p, d_c, stat,
     st_sib, r_sib, st_own, r_own, dq_out, dq_in,
     lens_in, in_sem, s1, r1, s2, r2, s3, r3, s4, r4, s5, r5, s6, r6,
 ):
@@ -123,22 +123,23 @@
 
     for load in loads[4:]:
         load.wait()
-    length = lens_in[0]
+    length = lens_in[0, 0]
 
     def scores(keys, values, q, gr, mask, e_ref, d_ref, rows, qs, qn):
         mx = jnp.full((8, qn), NEG, F)
         for c, r in enumerate(rows):
-            s = nt(keys(c), q)
+            k = keys(c)
+            s = nt(jnp.concatenate([k, k], axis=1), q)
             keep = mask(c)
             if keep is not None:
                 s = jnp.where(keep, s, NEG)
             sbuf[c % 4 * CB : c % 4 * CB + CB, c // 4 * qn : c // 4 * qn + qn] = s
             mx = jnp.maximum(mx, fold(s, jnp.max))
-        m = rowmax(mx) * SCALE2
+        m = rowmax(mx)
         l = jnp.zeros((8, qn), F)
         w = jnp.zeros((8, qn), F)
         for c, r in enumerate(rows):
-            e = jnp.exp2(sbuf[c % 4 * CB : c % 4 * CB + CB, c // 4 * qn : c // 4 * qn + qn] * SCALE2 - m)
+            e = jnp.exp2(sbuf[c % 4 * CB : c % 4 * CB + CB, c // 4 * qn : c // 4 * qn + qn] - m)
             e_ref[r, qs] = e.astype(B)
             dp = nt(values(c), gr).astype(B)
             d_ref[r, qs] = dp
@@ -155,6 +156,14 @@
 
     diagonal = lax.broadcasted_iota(jnp.int32, (CB, CB), 0) <= lax.broadcasted_iota(jnp.int32, (CB, CB), 1)
 
+    def split_scaled(rows):
+        scaled = q_all[rows, :].astype(F) * SCALE2
+        high = scaled.astype(B)
+        q_two[rows, 0:HS] = high
+        q_two[rows, HS:] = (scaled - high.astype(F)).astype(B)
+
+    split_scaled(slice(0, NC))
+
     def cont_rows(i):
         return [slice(j * CB, (j + 1) * CB) for j in range(i + 1)]
 
@@ -162,7 +171,7 @@
         rows = cont_rows(i)
         qs = rows[i]
         m, l, w = scores(
-            lambda c: k_c[rows[c], :], lambda c: v_c[rows[c], :], q_all[qs, :], g_all[qs, :],
+            lambda c: k_c[rows[c], :], lambda c: v_c[rows[c], :], q_two[qs, :], g_all[qs, :],
             lambda c: diagonal if c == i else None, e_c, d_c, rows, qs, CB,
         )
         stat[0, 0:1, qs] = m
@@ -195,7 +204,7 @@
     def prompt_scores(k, qs, qn, mask):
         rows = group_rows(k)
         m, l, w = scores(
-            lambda c: kv_rows(0, rows[c]), lambda c: kv_rows(1, rows[c]), q_all[qs, :], g_all[qs, :],
+            lambda c: kv_rows(0, rows[c]), lambda c: kv_rows(1, rows[c]), q_two[qs, :], g_all[qs, :],
             lambda c: mask(rows[c]), e_p, d_p, rows, qs, qn,
         )
         stat[k, 0:1, qs] = m
@@ -229,6 +238,7 @@
     remote(seven, seven, s2.at[0], r2.at[0], (p, sibling)).wait()
     q_all[own_rows, :] = qg[:, 0].reshape(PQ, HS)
     g_all[own_rows, :] = qg[:, 1].reshape(PQ, HS)
+    split_scaled(own_rows)
     prompt_scores(1, own_rows, PQ, prompt_mask)
     prompt_scores(2, own_rows, PQ, prompt_mask)
     for f in forwards:
@@ -267,12 +277,13 @@
         r = slice(start, start + size)
         return nn(d_p[r, :], q_all[...]) * SCALE, nn(e_p[r, :], g_all[...])
 
+    halves = 2
     units = 4
     unit = GK // units
     prompt_grads(3)
     to_sibling = []
-    for u in range(units):
-        dk, dv = parts(GK + u * unit, unit)
+    for u in range(halves):
+        dk, dv = parts(GK + u * 2 * unit, 2 * unit)
         st_sib[u, 0] = dk.astype(B)
         st_sib[u, 1] = dv.astype(B)
         c = remote(st_sib.at[u], r_sib.at[u], s4.at[u], r4.at[u], (p, sibling))
@@ -284,10 +295,12 @@
     per = CHIPS // units
     for u in range(units):
         dk, dv = parts(u * unit, unit)
-        to_sibling[u].wait_recv()
+        if u % 2 == 0:
+            to_sibling[u // 2].wait_recv()
         at = slice(u * per, (u + 1) * per)
-        st_own[at, :, 0] = (dk + r_sib[u, 0].astype(F)).astype(B).reshape(per, HEADS, 16, HS)
-        st_own[at, :, 1] = (dv + r_sib[u, 1].astype(F)).astype(B).reshape(per, HEADS, 16, HS)
+        share = slice(u % 2 * unit, u % 2 * unit + unit)
+        st_own[at, :, 0] = (dk + r_sib[u // 2, 0, share].astype(F)).astype(B).reshape(per, HEADS, 16, HS)
+        st_own[at, :, 1] = (dv + r_sib[u // 2, 1, share].astype(F)).astype(B).reshape(per, HEADS, 16, HS)
         for dc in range(u * per, (u + 1) * per):
             for dp in range(HEADS):
                 if dc or dp:
@@ -380,19 +393,20 @@
             vmem((HEADS, 2, 16, HS), B),
             vmem((HEADS, 2, 16, HS), B),
             vmem((HEADS, 2, 16, HS), B),
+            vmem((NQ, 2 * HS), B),
             vmem((GK, WB), F),
             vmem((NP, NQ), B),
             vmem((NC, NC), B),
             vmem((NP, NQ), B),
             vmem((NC, NC), B),
             vmem((4, 8, NQ), F),
-            vmem((4, 2, GK // 4, HS), B),
-            vmem((4, 2, GK // 4, HS), B),
+            vmem((2, 2, GK // 2, HS), B),
+            vmem((2, 2, GK // 2, HS), B),
             vmem((CHIPS, HEADS, 2, 16, HS), B),
             vmem((HEADS * CHIPS, 2, 16, HS), B),
             vmem((HEADS, 16, HS), B),
             vmem((HEADS, 16, HS), B),
-            pltpu.SMEM((1,), jnp.int32),
+            pltpu.SMEM((1, 1), jnp.int32),
             dma((9,)),
             dma((CHIPS,)),
             dma((CHIPS,)),
@@ -400,14 +414,14 @@
             dma((1,)),
             dma((CHIPS,)),
             dma((CHIPS,)),
-            dma((4,)),
-            dma((4,)),
+            dma((2,)),
+            dma((2,)),
         ]
         + [dma((1,))] * 4,
         compiler_params=pltpu.CompilerParams(
             collective_id=0, has_side_effects=True, vmem_limit_bytes=58 * 2**20
         ),
-    )(prompt_q, prompt_k, prompt_v, prompt_grad, cont_q, cont_k, cont_v, cont_grad, lengths)
+    )(prompt_q, prompt_k, prompt_v, prompt_grad, cont_q, cont_k, cont_v, cont_grad, lengths.reshape(1, 1))
     return pl.pallas_call(
         hand_over,
         out_shape=[jax.ShapeDtypeStruct(shape, B) for shape in shapes],

time: 48.8 us -> 47.2 us (0.967)
  Pallas kernels: 47.1 us -> 45.2 us
    pallas_call x1, Pallas kernels: 45.9 us -> 44 us  [shards(): pl.pallas_call(kernel, out_shape=[vmem(shape, B) for shape in shapes], in...]
where the time goes in v4:
time: 47.2 us; the launch traced here: 46.7 us
  Pallas kernels  45.2 us (96%)
  between operations  1.47 us (3%)
    pallas_call x1, Pallas kernels, shards(): pl.pallas_call(kernel, out_shape=[vmem(shape, B) for shape in shapes], in...  44 us
    pallas_call x1, Pallas kernels, shards(): pl.pallas_call(hand_over, out_shape=[jax.ShapeDtypeStruct(shape, B) for s...  1.23 us

profile of v4, /device:TPU:1, one launch (start us, length us, event | category | flops | bytes accessed | tf_op | source)
XLA Modules:
  0.0 46.7 jit_solution(16239874098462893163)
XLA Ops:
  1.3 44.0 %shard_map.136 = (bf16[16,1024]{1,0:T(8,128)(2,1)S(1)}, bf16[16,1024]{1,0:T(8,128)(2,1)S(1)}, bf16[16,1024]{1,0:T(8,128)(2,1)S(1)}, bf16[1,2048,128]{2,1,0:T(8,1...) custom-call(bf16[16,1024]{1,0:T(8,128)(2,1)} %pq.1, bf16[16,1024]{1,0:T(8,128)(2,1)} %pk.1, ...), custom_call_target="tpu_custom_call" | custom-call | tf_op jit(solution)/shard_map/pallas_call | solution.py:379
  45.3 1.2 %shard_map.137 = (bf16[16,1024]{1,0:T(8,128)(2,1)}, bf16[16,1024]{1,0:T(8,128)(2,1)}, bf16[16,1024]{1,0:T(8,128)(2,1)}, bf16[1,2048,128]{2,1,0:T(8,128)(2,1)}, b...) custom-call(bf16[16,1024]{1,0:T(8,128)(2,1)S(1)} %get-tuple-element.12.refs_0_, ...), custom_call_target="tpu_custom_call" | custom-call | tf_op jit(solution)/shard_map/pallas_call | solution.py:425

commit v5 on v4

--- a/solution.py
+++ b/solution.py
@@ -125,6 +125,9 @@
         load.wait()
     length = lens_in[0, 0]
 
+    def place(c, qn):
+        return slice(c % 4 * CB, c % 4 * CB + CB), slice(c // 4 * qn, c // 4 * qn + qn)
+
     def scores(keys, values, q, gr, mask, e_ref, d_ref, rows, qs, qn):
         mx = jnp.full((8, qn), NEG, F)
         for c, r in enumerate(rows):
@@ -133,13 +136,13 @@
             keep = mask(c)
             if keep is not None:
                 s = jnp.where(keep, s, NEG)
-            sbuf[c % 4 * CB : c % 4 * CB + CB, c // 4 * qn : c // 4 * qn + qn] = s
+            sbuf[place(c, qn)] = s
             mx = jnp.maximum(mx, fold(s, jnp.max))
         m = rowmax(mx)
         l = jnp.zeros((8, qn), F)
         w = jnp.zeros((8, qn), F)
         for c, r in enumerate(rows):
-            e = jnp.exp2(sbuf[c % 4 * CB : c % 4 * CB + CB, c // 4 * qn : c // 4 * qn + qn] - m)
+            e = jnp.exp2(sbuf[place(c, qn)] - m)
             e_ref[r, qs] = e.astype(B)
             dp = nt(values(c), gr).astype(B)
             d_ref[r, qs] = dp
@@ -195,7 +198,7 @@
         first = r.start // HS
         return kv[first // CHIPS, first % CHIPS : first % CHIPS + CB // HS, :, which].reshape(CB, HS)
 
-    groups = {1: (0, GK // 2), 2: (GK // 2, GK), 3: (GK, NP)}
+    groups = {k + 1: (k * GK // 2, (k + 1) * GK // 2) for k in range(4)}
     own_rows = slice(NC, NQ)
 
     def group_rows(k):
@@ -231,6 +234,9 @@
     for dc in range(CHIPS // 2):
         forward(dc)
     member_scores(1)
+    for dc in range(CHIPS // 2):
+        forwards[dc].wait_recv()
+    member_scores(3)
     for dc in range(CHIPS // 2, CHIPS):
         forward(dc)
     member_scores(2)
@@ -239,28 +245,30 @@
     q_all[own_rows, :] = qg[:, 0].reshape(PQ, HS)
     g_all[own_rows, :] = qg[:, 1].reshape(PQ, HS)
     split_scaled(own_rows)
-    prompt_scores(1, own_rows, PQ, prompt_mask)
-    prompt_scores(2, own_rows, PQ, prompt_mask)
-    for f in forwards:
-        f.wait_recv()
-    member_scores(3)
-    prompt_scores(3, own_rows, PQ, prompt_mask)
+    for k in (1, 2, 3):
+        prompt_scores(k, own_rows, PQ, prompt_mask)
+    for dc in range(CHIPS // 2, CHIPS):
+        forwards[dc].wait_recv()
+    member_scores(4)
+    prompt_scores(4, own_rows, PQ, prompt_mask)
 
     stat[0, 0:1, own_rows] = jnp.full((1, PQ), NEG, F)
     stat[0, 1:3, own_rows] = jnp.zeros((2, PQ), F)
     for i in range(NQ // PQ):
         qs = slice(i * PQ, (i + 1) * PQ)
-        ms = [stat[k, 0:1, qs] for k in range(4)]
-        top = jnp.maximum(jnp.maximum(ms[0], ms[1]), jnp.maximum(ms[2], ms[3]))
+        ms = [stat[k, 0:1, qs] for k in range(5)]
+        top = ms[0]
+        for m in ms[1:]:
+            top = jnp.maximum(top, m)
         scale = [jnp.exp2(m - top) for m in ms]
-        l = sum(scale[k] * stat[k, 1:2, qs] for k in range(4))
-        w = sum(scale[k] * stat[k, 2:3, qs] for k in range(4))
+        l = sum(scale[k] * stat[k, 1:2, qs] for k in range(5))
+        w = sum(scale[k] * stat[k, 2:3, qs] for k in range(5))
         inv = 1.0 / l
         delta = w * inv
         if i < NC // PQ:
             live = (lax.broadcasted_iota(jnp.int32, (1, PQ), 1) + i * PQ) < length
             inv = jnp.where(live, inv, 0.0)
-        for k in range(4):
+        for k in range(5):
             stat[k, 3:4, qs] = scale[k] * inv
         stat[0, 4:5, qs] = delta
 
@@ -281,6 +289,7 @@
     units = 4
     unit = GK // units
     prompt_grads(3)
+    prompt_grads(4)
     to_sibling = []
     for u in range(halves):
         dk, dv = parts(GK + u * 2 * unit, 2 * unit)
@@ -399,7 +408,7 @@
             vmem((NC, NC), B),
             vmem((NP, NQ), B),
             vmem((NC, NC), B),
-            vmem((4, 8, NQ), F),
+            vmem((5, 8, NQ), F),
             vmem((2, 2, GK // 2, HS), B),
             vmem((2, 2, GK // 2, HS), B),
             vmem((CHIPS, HEADS, 2, 16, HS), B),
@@ -419,7 +428,7 @@
         ]
         + [dma((1,))] * 4,
         compiler_params=pltpu.CompilerParams(
-            collective_id=0, has_side_effects=True, vmem_limit_bytes=58 * 2**20
+            collective_id=0, has_side_effects=True, vmem_limit_bytes=60 * 2**20
         ),
     )(prompt_q, prompt_k, prompt_v, prompt_grad, cont_q, cont_k, cont_v, cont_grad, lengths.reshape(1, 1))
     return pl.pallas_call(

time: 47.2 us -> 46.6 us (0.987)
  no operation moved by 1% of the time
where the time goes in v5:
time: 46.6 us; the launch traced here: 46.4 us
  Pallas kernels  44.9 us (96%)
  between operations  1.47 us (3%)
    pallas_call x1, Pallas kernels, shards(): pl.pallas_call(kernel, out_shape=[vmem(shape, B) for shape in shapes], in...  43.7 us
    pallas_call x1, Pallas kernels, shards(): pl.pallas_call(hand_over, out_shape=[jax.ShapeDtypeStruct(shape, B) for s...  1.23 us

profile of v5, /device:TPU:1, one launch (start us, length us, event | category | flops | bytes accessed | tf_op | source)
XLA Modules:
  0.0 46.4 jit_solution(2433973660991349057)
XLA Ops:
  1.3 43.7 %shard_map.136 = (bf16[16,1024]{1,0:T(8,128)(2,1)S(1)}, bf16[16,1024]{1,0:T(8,128)(2,1)S(1)}, bf16[16,1024]{1,0:T(8,128)(2,1)S(1)}, bf16[1,2048,128]{2,1,0:T(8,1...) custom-call(bf16[16,1024]{1,0:T(8,128)(2,1)} %pq.1, bf16[16,1024]{1,0:T(8,128)(2,1)} %pk.1, ...), custom_call_target="tpu_custom_call" | custom-call | tf_op jit(solution)/shard_map/pallas_call | solution.py:388
  45.0 1.2 %shard_map.137 = (bf16[16,1024]{1,0:T(8,128)(2,1)}, bf16[16,1024]{1,0:T(8,128)(2,1)}, bf16[16,1024]{1,0:T(8,128)(2,1)}, bf16[1,2048,128]{2,1,0:T(8,128)(2,1)}, b...) custom-call(bf16[16,1024]{1,0:T(8,128)(2,1)S(1)} %get-tuple-element.12.refs_0_, ...), custom_call_target="tpu_custom_call" | custom-call | tf_op jit(solution)/shard_map/pallas_call | solution.py:434

commit v6 on v5

--- a/solution.py
+++ b/solution.py
@@ -126,7 +126,7 @@
     length = lens_in[0, 0]
 
     def place(c, qn):
-        return slice(c % 4 * CB, c % 4 * CB + CB), slice(c // 4 * qn, c // 4 * qn + qn)
+        return slice(c % 2 * CB, c % 2 * CB + CB), slice(c // 2 * qn, c // 2 * qn + qn)
 
     def scores(keys, values, q, gr, mask, e_ref, d_ref, rows, qs, qn):
         mx = jnp.full((8, qn), NEG, F)
@@ -215,11 +215,7 @@
         stat[k, 2:3, qs] = w
 
     def member_scores(k):
-        def body(i, carry):
-            prompt_scores(k, pl.ds(pl.multiple_of(i * WB, WB), WB), WB, lambda r: None)
-            return carry
-
-        lax.fori_loop(0, NC // WB, body, 0)
+        prompt_scores(k, slice(0, NC), NC, lambda r: None)
 
     def prompt_mask(r):
         row = lax.broadcasted_iota(jnp.int32, (CB, 1), 0)
@@ -403,7 +399,7 @@
             vmem((HEADS, 2, 16, HS), B),
             vmem((HEADS, 2, 16, HS), B),
             vmem((NQ, 2 * HS), B),
-            vmem((GK, WB), F),
+            vmem((2 * CB, NC), F),
             vmem((NP, NQ), B),
             vmem((NC, NC), B),
             vmem((NP, NQ), B),

time: 46.6 us -> 46.1 us (0.989)
  no operation moved by 1% of the time
where the time goes in v6:
time: 46.1 us; the launch traced here: 46 us
  Pallas kernels  44.5 us (97%)
  between operations  1.45 us (3%)
    pallas_call x1, Pallas kernels, shards(): pl.pallas_call(kernel, out_shape=[vmem(shape, B) for shape in shapes], in...  43.3 us
    pallas_call x1, Pallas kernels, shards(): pl.pallas_call(hand_over, out_shape=[jax.ShapeDtypeStruct(shape, B) for s...  1.23 us

profile of v6, /device:TPU:1, one launch (start us, length us, event | category | flops | bytes accessed | tf_op | source)
XLA Modules:
  0.0 46.0 jit_solution(13794182221017264007)
XLA Ops:
  1.3 43.3 %shard_map.136 = (bf16[16,1024]{1,0:T(8,128)(2,1)S(1)}, bf16[16,1024]{1,0:T(8,128)(2,1)S(1)}, bf16[16,1024]{1,0:T(8,128)(2,1)S(1)}, bf16[1,2048,128]{2,1,0:T(8,1...) custom-call(bf16[16,1024]{1,0:T(8,128)(2,1)} %pq.1, bf16[16,1024]{1,0:T(8,128)(2,1)} %pk.1, ...), custom_call_target="tpu_custom_call" | custom-call | tf_op jit(solution)/shard_map/pallas_call | solution.py:384
  44.6 1.2 %shard_map.137 = (bf16[16,1024]{1,0:T(8,128)(2,1)}, bf16[16,1024]{1,0:T(8,128)(2,1)}, bf16[16,1024]{1,0:T(8,128)(2,1)}, bf16[1,2048,128]{2,1,0:T(8,128)(2,1)}, b...) custom-call(bf16[16,1024]{1,0:T(8,128)(2,1)S(1)} %get-tuple-element.12.refs_0_, ...), custom_call_target="tpu_custom_call" | custom-call | tf_op jit(solution)/shard_map/pallas_call | solution.py:430
